TPU v7x, 32 devices: a whole 2x2x4 slice. The times are simulated.
32 devices in a mesh: groups: 2 (over x), rows: 16 (over z, y, core).
Axes of the slice: x: 2, y: 2, z: 4, core: 2. Of those that a mesh axis runs over, the one named last changes fastest.
Arguments:
- local_tiles: bfloat16 [8192, 128, 128], P(('groups', 'rows')), parts along dimension 0, may hold values from 0 to 1, as said below
- local_row: int32 [8192], P(('groups', 'rows')), parts along dimension 0, may hold values from 0 to 15, as said below
- local_col: int32 [8192], P(('groups', 'rows')), parts along dimension 0, may hold values from 0 to 15, as said below
- local_count: int32 [32], P(('groups', 'rows')), parts along dimension 0, may hold values from 128 to 256, as said below
- remote_tiles: bfloat16 [512, 4, 128, 128], P(('groups', 'rows')), parts along dimension 0, may hold values from 0 to 1, as said below
- remote_row: int32 [512, 4], P(('groups', 'rows')), parts along dimension 0, may hold values from 0 to 15, as said below
- remote_col: int32 [512, 4], P(('groups', 'rows')), parts along dimension 0, may hold values from 0 to 15, as said below
- remote_count: int32 [512], P(('groups', 'rows')), parts along dimension 0, may hold values from 0 to 4, as said below
- start_basis: float32 [128, 32768], P('groups', 'rows'), parts along dimension 0, may hold values from -6 to 6
- start_dir: float32 [128, 32768], P('groups', 'rows'), parts along dimension 0, may hold values from -4 to 4
- coeffs: float32 [4, 64, 192], P('groups'), parts along dimension 0, may hold values from -4 to 4, as said below
Outputs:
- ortho_out: float32 [128, 32768], P('groups', 'rows'), parts along dimension 0
- residual_out: float32 [128, 32768], P('groups', 'rows'), parts along dimension 0
- projected_out: float32 [128, 64], P('groups'), parts along dimension 0
There are 2 independent parts, one for each index of `groups`. A program takes and returns all parts, laid end to end along the dimension named above; each array names one. Nothing has to cross between parts.
Inputs may be any that keep to these rules, and one draw needn't show every extreme that they name: `local_tiles`: entries are 0 or between 0.25 and 1; slots past the live counts hold values that must be ignored. `remote_tiles`: entries are 0 or between 0.25 and 1; slots past the live counts hold values that must be ignored. `local_row`: block index on the owning device; slots 0 to 15 of each device hold its diagonal tiles. `local_col`: block index on the same device. `local_count`: some device has all 256 slots live in every draw. `remote_row`: block index on the owning device. `remote_col`: block index on the peer. `remote_count`: 0 toward the device itself, at least 1 toward every other peer; every device has some peer with exactly 4. `coeffs`: the basis part is the identity plus off-diagonal and diagonal perturbations of magnitude at most 0.15.
All inputs are finite; a program needn't handle non-finite values.
Results may differ from a plain program's by a relative error of at most 0.00086.
Values may be sent and summed in bfloat16 or wider, within the bound.
A program may use at most 192 MiB of HBM per device.

v0:
```python
import jax
import jax.numpy as jnp
from jax import lax
from jax.sharding import PartitionSpec as P

highest = lax.Precision.HIGHEST


def add_blocks(values, block_ids, blocks):
    selector = (jnp.arange(blocks, dtype=jnp.int32)[:, None] == block_ids[None, :]).astype(
        jnp.float32
    )
    flat = values.reshape(values.shape[0], -1)
    summed = jnp.dot(selector, flat, precision=highest, preferred_element_type=jnp.float32)
    return summed.reshape((blocks,) + values.shape[1:])


def shards(
    local_tiles,
    local_row,
    local_col,
    local_count,
    remote_tiles,
    remote_row,
    remote_col,
    remote_count,
    start_basis,
    start_dir,
    coeffs,
):
    tile_edge = local_tiles.shape[1]
    columns = start_basis.shape[0]
    blocks = start_basis.shape[1] // tile_edge
    slots = remote_tiles.shape[1]
    node_total = start_basis.shape[1] * lax.axis_size("rows")
    live_local = (jnp.arange(local_tiles.shape[0]) < local_count[0]).astype(jnp.float32)
    live_far = (jnp.arange(slots)[None, :] < remote_count[:, None]).astype(jnp.float32)
    wanted_col, wanted_count = (
        lax.all_to_all(remote_col, "rows", split_axis=0, concat_axis=0, tiled=True),
        lax.all_to_all(remote_count, "rows", split_axis=0, concat_axis=0, tiled=True),
    )
    flat_rows = remote_row.reshape(-1)
    flat_wanted = wanted_col.reshape(-1)
    row_sums = jnp.sum(local_tiles, axis=2, dtype=jnp.float32) * live_local[:, None]
    col_sums = jnp.sum(local_tiles, axis=1, dtype=jnp.float32) * live_local[:, None]
    far_rowsum = jnp.sum(remote_tiles, axis=3, dtype=jnp.float32) * live_far[:, :, None]
    degree = add_blocks(row_sums, local_row, blocks) + add_blocks(col_sums, local_col, blocks)
    degree = degree + add_blocks(far_rowsum.reshape(-1, tile_edge), flat_rows, blocks)
    far_colsum = jnp.sum(remote_tiles, axis=2, dtype=jnp.float32) * live_far[:, :, None]
    far_sums = lax.all_to_all(far_colsum, "rows", split_axis=0, concat_axis=0, tiled=True)
    degree = degree + add_blocks(far_sums.reshape(-1, tile_edge), flat_wanted, blocks)
    degree = 0.5 * degree.reshape(-1)
    basis = start_basis
    direction = start_dir
    identity = jnp.eye(columns, dtype=jnp.float32)
    passes = coeffs.shape[0]
    for iteration in range(passes + 1):
        basis_bf = basis.astype(jnp.bfloat16).reshape(columns, blocks, tile_edge).transpose(1, 0, 2)
        near_part = (
            jnp.einsum(
                "tij,tkj->tki", local_tiles, basis_bf[local_col], preferred_element_type=jnp.float32
            )
            * live_local[:, None, None]
        )
        back_part = (
            jnp.einsum(
                "tji,tkj->tki", local_tiles, basis_bf[local_row], preferred_element_type=jnp.float32
            )
            * live_local[:, None, None]
        )
        summed = add_blocks(near_part, local_row, blocks) + add_blocks(back_part, local_col, blocks)
        fetched = lax.all_to_all(
            basis_bf[wanted_col], "rows", split_axis=0, concat_axis=0, tiled=True
        )
        returned = (
            jnp.einsum(
                "ecji,eckj->ecki",
                remote_tiles,
                basis_bf[remote_row],
                preferred_element_type=jnp.float32,
            )
            * live_far[:, :, None, None]
        )
        incoming = lax.all_to_all(returned, "rows", split_axis=0, concat_axis=0, tiled=True)
        ahead_part = (
            jnp.einsum("ecij,eckj->ecki", remote_tiles, fetched, preferred_element_type=jnp.float32)
            * live_far[:, :, None, None]
        )
        summed = summed + add_blocks(ahead_part.reshape(-1, columns, tile_edge), flat_rows, blocks)
        summed = summed + add_blocks(incoming.reshape(-1, columns, tile_edge), flat_wanted, blocks)
        summed = summed.transpose(1, 0, 2).reshape(columns, -1)
        image = degree[None, :] * basis - 0.5 * summed
        gram_part = jnp.dot(basis, basis.T, precision=highest, preferred_element_type=jnp.float32)
        cross_part = jnp.dot(image, basis.T, precision=highest, preferred_element_type=jnp.float32)
        gram_sum, cross_sum = lax.psum((gram_part, cross_part), "rows")
        gram_now = gram_sum / node_total
        cross_now = cross_sum / node_total
        lower_chol = jnp.linalg.cholesky(gram_now)
        lower_inv = jax.scipy.linalg.solve_triangular(lower_chol, identity, lower=True)
        ortho = jnp.dot(lower_inv, basis, precision=highest, preferred_element_type=jnp.float32)
        image_ortho = jnp.dot(
            lower_inv, image, precision=highest, preferred_element_type=jnp.float32
        )
        projected = jnp.dot(
            jnp.dot(lower_inv, cross_now, precision=highest, preferred_element_type=jnp.float32),
            lower_inv.T,
            precision=highest,
            preferred_element_type=jnp.float32,
        )
        residual = (
            image_ortho
            - jnp.dot(projected, ortho, precision=highest, preferred_element_type=jnp.float32)
        ) / (1.0 + degree)[None, :]
        if iteration < passes:
            coeff_now = coeffs[iteration]
            direction = jnp.dot(
                coeff_now[:, columns : 2 * columns],
                residual,
                precision=highest,
                preferred_element_type=jnp.float32,
            ) + jnp.dot(
                coeff_now[:, 2 * columns :],
                direction,
                precision=highest,
                preferred_element_type=jnp.float32,
            )
            basis = (
                jnp.dot(
                    coeff_now[:, :columns],
                    ortho,
                    precision=highest,
                    preferred_element_type=jnp.float32,
                )
                + direction
            )
    return (ortho, residual, projected)


def solution(mesh):
    placed = (
        P(("groups", "rows"), None, None),
        P(("groups", "rows")),
        P(("groups", "rows")),
        P(("groups", "rows")),
        P(("groups", "rows"), None, None, None),
        P(("groups", "rows"), None),
        P(("groups", "rows"), None),
        P(("groups", "rows")),
        P("groups", "rows"),
        P("groups", "rows"),
        P("groups", None, None),
    )
    return jax.shard_map(
        shards,
        mesh=mesh,
        in_specs=placed,
        out_specs=(P("groups", "rows"), P("groups", "rows"), P("groups", None)),
        check_vma=False,
    )
```

profile of v0, /device:TPU:0, one launch (start us, length us, event | category | flops | bytes accessed | tf_op | source)
XLA Modules:
  0.0 627.0 jit_solution(1479047889713349670)
XLA Ops:
  2.1 7.4 %all-to-all-start = ((s32[16,1,4]{2,1,0:T(1,128)}), s32[16,1,4]{2,1,0:T(1,128)S(1)}, u32[]{:S(2)}, u32[]{:S(2)}) async-start(s32[16,1,4]{2,1,0:T(1,128)} %copy.90), calls=%async_computation | async-start | bytes 16384 | tf_op jit(solution)/shard_map/all_to_all | solution.py:39
  15.8 5.9 all-to-all-start.1
  35.7 10.5 %broadcast_multiply_fusion.5 = f32[256,64,128]{2,1,0:T(8,128)S(1)} fusion(f32[256]{0:T(256)S(1)} %compare_convert_fusion, bf16[256,64,128]{2,1,0:T(8,128)(2,1)} %gather_fusion, bf16[256,128,128]{2,1,0:T(8,128)(2,1)} %param.14), kind=kOutput, calls=%fused_computation.27 | convolution fusion | flops 538968064 | bytes 20972544 | tf_op jit(solution)/shard_map/tij,tkj->tki/dot_general | solution.py:60
  46.2 10.9 %copy.229 = f32[32,8,64,128]{3,1,2,0:T(8,128)} copy(f32[32,8,64,128]{3,2,1,0:T(8,128)S(1)} %bitcast.347) | data formatting | bytes 16777216
  57.1 9.5 %copy.92 = f32[8192,256]{1,0:T(8,128)} copy(f32[8192,256]{0,1:T(8,128)} %bitcast.348) | data formatting | bytes 16777216 | tf_op jit(solution)/shard_map/dot_general | solution.py:14
  74.9 6.0 all-to-all-start.3
  80.9 7.0 %broadcast_multiply_fusion.4 = f32[256,64,128]{2,1,0:T(8,128)S(1)} fusion(f32[256]{0:T(256)S(1)} %compare_convert_fusion, bf16[256,64,128]{2,1,0:T(8,128)(2,1)} %gather_fusion.1, bf16[256,128,128]{2,1,0:T(8,128)(2,1)} %param.14), kind=kOutput, calls=%fused_computation.26 | convolution fusion | flops 538968064 | bytes 20972544 | tf_op jit(solution)/shard_map/tji,tkj->tki/dot_general | solution.py:66
  87.9 10.9 %copy.228 = f32[32,8,64,128]{3,1,2,0:T(8,128)} copy(f32[32,8,64,128]{3,2,1,0:T(8,128)S(1)} %bitcast.339) | data formatting | bytes 16777216
  98.8 9.2 %copy.93 = f32[8192,256]{1,0:T(8,128)} copy(f32[8192,256]{0,1:T(8,128)} %bitcast.349) | data formatting | bytes 16777216 | tf_op jit(solution)/shard_map/dot_general | solution.py:14
  115.2 6.3 %fusion.113 = f32[16,64,128]{2,0,1:T(8,128)S(1)} fusion(f32[64,128,256]{2,1,0:T(8,128)} %bitcast.341, s32[256]{0:T(256)S(1)} %copy-done.15), kind=kOutput, calls=%fused_computation.166 | convolution fusion | flops 402657280 | bytes 8913920 | tf_op jit(solution)/shard_map/dot_general | solution.py:14
  140.3 62.2 %all-reduce.2 = (f32[64,64]{0,1:T(8,128)S(1)}, f32[64,64]{0,1:T(8,128)S(1)}) all-reduce(f32[64,64]{0,1:T(8,128)S(1)} %fusion.146, f32[64,64]{0,1:T(8,128)S(1)} %fusion.52), channel_id=1, replica_groups=mesh['groups'=2,'rows'=16] {'rows'}, use_global_device_ids=true, to_apply=%region_0.0 | all-reduce | flops 8192 | bytes 65536 | tf_op jit(solution)/shard_map/psum | solution.py:95
  202.7 5.8 cholesky.59
  232.0 18.0 %all-to-all-done.4 = bf16[16,4,64,128]{3,2,1,0:T(8,128)(2,1)} async-done(((bf16[16,4,64,128]{3,2,1,0:T(8,128)(2,1)}), bf16[16,4,64,128]{3,2,1,0:T(8,128)(2,1)}, u32[]{:S(2)}, u32[]{:S(2)}) %all-to-all-start.4) | async-done | bytes 1048608 | tf_op jit(solution)/shard_map/all_to_all | solution.py:72
  250.0 7.3 %all-to-all-start.5 = ((f32[16,4,64,128]{3,2,1,0:T(8,128)}), f32[16,4,64,128]{3,2,1,0:T(8,128)}, u32[]{:S(2)}, u32[]{:S(2)}) async-start(f32[16,4,64,128]{3,2,1,0:T(8,128)} %convolution_multiply_fusion.2), calls=%async_computation.5 | async-start | bytes 4194304 | tf_op jit(solution)/shard_map/all_to_all | solution.py:84
  263.3 10.5 %broadcast_multiply_fusion.3 = f32[256,64,128]{2,1,0:T(8,128)S(1)} fusion(f32[256]{0:T(256)S(1)} %compare_convert_fusion, bf16[256,64,128]{2,1,0:T(8,128)(2,1)} %gather_fusion.4, bf16[256,128,128]{2,1,0:T(8,128)(2,1)} %param.14), kind=kOutput, calls=%fused_computation.25 | convolution fusion | flops 538968064 | bytes 20972544 | tf_op jit(solution)/shard_map/tij,tkj->tki/dot_general | solution.py:60
  273.8 10.9 %copy.227 = f32[32,8,64,128]{3,1,2,0:T(8,128)} copy(f32[32,8,64,128]{3,2,1,0:T(8,128)S(1)} %bitcast.350) | data formatting | bytes 16777216
  284.7 9.2 %copy.103 = f32[8192,256]{1,0:T(8,128)} copy(f32[8192,256]{0,1:T(8,128)} %bitcast.351) | data formatting | bytes 16777216 | tf_op jit(solution)/shard_map/dot_general | solution.py:14
  293.8 7.0 %broadcast_multiply_fusion.2 = f32[256,64,128]{2,1,0:T(8,128)S(1)} fusion(f32[256]{0:T(256)S(1)} %compare_convert_fusion, bf16[256,64,128]{2,1,0:T(8,128)(2,1)} %gather_fusion.5, bf16[256,128,128]{2,1,0:T(8,128)(2,1)} %param.14), kind=kOutput, calls=%fused_computation.24 | convolution fusion | flops 538968064 | bytes 20972544 | tf_op jit(solution)/shard_map/tji,tkj->tki/dot_general | solution.py:66
  300.8 10.9 %copy.226 = f32[32,8,64,128]{3,1,2,0:T(8,128)} copy(f32[32,8,64,128]{3,2,1,0:T(8,128)S(1)} %bitcast.340) | data formatting | bytes 16777216
  311.7 9.0 %copy.104 = f32[8192,256]{1,0:T(8,128)} copy(f32[8192,256]{0,1:T(8,128)} %bitcast.352) | data formatting | bytes 16777216 | tf_op jit(solution)/shard_map/dot_general | solution.py:14
  321.3 6.5 %fusion.111 = f32[16,64,128]{2,0,1:T(8,128)S(1)} fusion(f32[64,128,256]{2,1,0:T(8,128)} %bitcast.344, s32[256]{0:T(256)S(1)} %copy-done.15), kind=kOutput, calls=%fused_computation.165 | convolution fusion | flops 402657280 | bytes 8913920 | tf_op jit(solution)/shard_map/dot_general | solution.py:14
  345.2 62.6 %all-reduce.1 = (f32[64,64]{0,1:T(8,128)S(1)}, f32[64,64]{0,1:T(8,128)S(1)}) all-reduce(f32[64,64]{0,1:T(8,128)S(1)} %fusion.149, f32[64,64]{0,1:T(8,128)S(1)} %fusion.54), channel_id=1, replica_groups=mesh['groups'=2,'rows'=16] {'rows'}, use_global_device_ids=true, to_apply=%region_8.0 | all-reduce | flops 8192 | bytes 65536 | tf_op jit(solution)/shard_map/psum | solution.py:95
  436.4 18.0 %all-to-all-done.6 = bf16[16,4,64,128]{3,2,1,0:T(8,128)(2,1)} async-done(((bf16[16,4,64,128]{3,2,1,0:T(8,128)(2,1)}), bf16[16,4,64,128]{3,2,1,0:T(8,128)(2,1)}, u32[]{:S(2)}, u32[]{:S(2)}) %all-to-all-start.6) | async-done | bytes 1048608 | tf_op jit(solution)/shard_map/all_to_all | solution.py:72
  454.4 7.0 %all-to-all-start.7 = ((f32[16,4,64,128]{3,2,1,0:T(8,128)}), f32[16,4,64,128]{3,2,1,0:T(8,128)}, u32[]{:S(2)}, u32[]{:S(2)}) async-start(f32[16,4,64,128]{3,2,1,0:T(8,128)} %convolution_multiply_fusion), calls=%async_computation.7 | async-start | bytes 4194304 | tf_op jit(solution)/shard_map/all_to_all | solution.py:84
  467.5 10.5 %broadcast_multiply_fusion.1 = f32[256,64,128]{2,1,0:T(8,128)S(1)} fusion(f32[256]{0:T(256)S(1)} %compare_convert_fusion, bf16[256,64,128]{2,1,0:T(8,128)(2,1)} %gather_fusion.8, bf16[256,128,128]{2,1,0:T(8,128)(2,1)} %param.14), kind=kOutput, calls=%fused_computation.23 | convolution fusion | flops 538968064 | bytes 20972544 | tf_op jit(solution)/shard_map/tij,tkj->tki/dot_general | solution.py:60
  478.0 10.9 %copy.225 = f32[32,8,64,128]{3,1,2,0:T(8,128)} copy(f32[32,8,64,128]{3,2,1,0:T(8,128)S(1)} %bitcast.353) | data formatting | bytes 16777216
  488.9 9.2 %copy.111 = f32[8192,256]{1,0:T(8,128)} copy(f32[8192,256]{0,1:T(8,128)} %bitcast.354) | data formatting | bytes 16777216 | tf_op jit(solution)/shard_map/dot_general | solution.py:14
  498.1 7.0 %broadcast_multiply_fusion = f32[256,64,128]{2,1,0:T(8,128)S(1)} fusion(f32[256]{0:T(256)S(1)} %compare_convert_fusion, bf16[256,64,128]{2,1,0:T(8,128)(2,1)} %gather_fusion.9, bf16[256,128,128]{2,1,0:T(8,128)(2,1)} %param.14), kind=kOutput, calls=%fused_computation.22 | convolution fusion | flops 538968064 | bytes 20972544 | tf_op jit(solution)/shard_map/tji,tkj->tki/dot_general | solution.py:66
  505.1 10.9 %copy.224 = f32[32,8,64,128]{3,1,2,0:T(8,128)} copy(f32[32,8,64,128]{3,2,1,0:T(8,128)S(1)} %bitcast.338) | data formatting | bytes 16777216
  515.9 9.0 %copy.112 = f32[8192,256]{1,0:T(8,128)} copy(f32[8192,256]{0,1:T(8,128)} %bitcast.355) | data formatting | bytes 16777216 | tf_op jit(solution)/shard_map/dot_general | solution.py:14
  525.5 6.7 %fusion.109 = f32[16,64,128]{2,0,1:T(8,128)S(1)} fusion(f32[64,128,256]{2,1,0:T(8,128)} %bitcast.343, s32[256]{0:T(256)S(1)} %copy-done.15), kind=kOutput, calls=%fused_computation.164 | convolution fusion | flops 402657280 | bytes 8913920 | tf_op jit(solution)/shard_map/dot_general | solution.py:14
  548.9 62.3 %all-reduce = (f32[64,64]{0,1:T(8,128)S(1)}, f32[64,64]{0,1:T(8,128)S(1)}) all-reduce(f32[64,64]{0,1:T(8,128)S(1)} %fusion.152, f32[64,64]{0,1:T(8,128)S(1)} %fusion.56), channel_id=1, replica_groups=mesh['groups'=2,'rows'=16] {'rows'}, use_global_device_ids=true, to_apply=%region_10.13 | all-reduce | flops 8192 | bytes 65536 | tf_op jit(solution)/shard_map/psum | solution.py:95
  (158 shorter events, 170.0 us)
Async XLA Ops:
  0.6 218.3 %copy-start = (f32[64,2048]{1,0:T(8,128)S(1)}, f32[64,2048]{1,0:T(8,128)}, u32[]{:S(2)}) copy-start(f32[64,2048]{1,0:T(8,128)} %param.23) | copy-start | bytes 1572868
  2.1 13.7 %all-to-all-start = ((s32[16,1,4]{2,1,0:T(1,128)}), s32[16,1,4]{2,1,0:T(1,128)S(1)}, u32[]{:S(2)}, u32[]{:S(2)}) async-start(s32[16,1,4]{2,1,0:T(1,128)} %copy.90), calls=%async_computation | async-start | bytes 16384 | tf_op jit(solution)/shard_map/all_to_all | solution.py:39
  15.8 12.6 %all-to-all-start.1 = ((f32[16,4,128]{2,1,0:T(4,128)}), f32[16,4,128]{2,1,0:T(4,128)S(1)}, u32[]{:S(2)}, u32[]{:S(2)}) async-start(f32[16,4,128]{2,1,0:T(4,128)} %broadcast_multiply_fusion.6), calls=%async_computation.1 | async-start | bytes 65536 | tf_op jit(solution)/shard_map/all_to_all | solution.py:50
  28.3 46.6 %all-to-all-start.2 = ((bf16[16,4,64,128]{3,2,1,0:T(8,128)(2,1)}), bf16[16,4,64,128]{3,2,1,0:T(8,128)(2,1)}, u32[]{:S(2)}, u32[]{:S(2)}) async-start(bf16[16,4,64,128]{3,2,1,0:T(8,128)(2,1)} %bitcast.19), calls=%async_computation.2 | async-start | bytes 2097152 | tf_op jit(solution)/shard_map/all_to_all | solution.py:72
  57.1 9.5 %copy-start.15 = (s32[256]{0:T(256)S(1)}, s32[256]{0:T(256)}, u32[]{:S(2)}) copy-start(s32[256]{0:T(256)} %param.15) | copy-start | bytes 3076
  66.6 3.1 copy-start.17
  66.6 5.0 copy-start.2
  74.9 56.9 %all-to-all-start.3 = ((f32[16,4,64,128]{3,2,1,0:T(8,128)}), f32[16,4,64,128]{3,2,1,0:T(8,128)}, u32[]{:S(2)}, u32[]{:S(2)}) async-start(f32[16,4,64,128]{3,2,1,0:T(8,128)} %convolution_multiply_fusion.4), calls=%async_computation.3 | async-start | bytes 4194304 | tf_op jit(solution)/shard_map/all_to_all | solution.py:84
  108.0 6.1 copy-start.16
  108.0 6.6 %copy-start.13 = (f32[2,64,192]{2,1,0:T(8,128)S(1)}, f32[2,64,192]{2,1,0:T(8,128)}, u32[]{:S(2)}) copy-start(f32[2,64,192]{2,1,0:T(8,128)} %param.24) | copy-start | bytes 294916
  108.0 6.6 %copy-start.6 = (f32[64,2048]{1,0:T(8,128)S(1)}, f32[64,2048]{1,0:T(8,128)}, u32[]{:S(2)}) copy-start(f32[64,2048]{1,0:T(8,128)} %param.22) | copy-start | bytes 1572868
  115.2 6.3 %copy-start.3 = (f32[8192,256]{1,0:T(8,128)S(1)}, f32[8192,256]{1,0:T(8,128)}, u32[]{:S(2)}) copy-start(f32[8192,256]{1,0:T(8,128)} %copy.93) | copy-start | bytes 25165828
  138.8 0.8 copy-start.9
  219.5 0.8 copy-start.7
  222.7 27.3 %all-to-all-start.4 = ((bf16[16,4,64,128]{3,2,1,0:T(8,128)(2,1)}), bf16[16,4,64,128]{3,2,1,0:T(8,128)(2,1)}, u32[]{:S(2)}, u32[]{:S(2)}) async-start(bf16[16,4,64,128]{3,2,1,0:T(8,128)(2,1)} %bitcast.369), calls=%async_computation.4 | async-start | bytes 2097152 | tf_op jit(solution)/shard_map/all_to_all | solution.py:72
  250.0 86.7 %all-to-all-start.5 = ((f32[16,4,64,128]{3,2,1,0:T(8,128)}), f32[16,4,64,128]{3,2,1,0:T(8,128)}, u32[]{:S(2)}, u32[]{:S(2)}) async-start(f32[16,4,64,128]{3,2,1,0:T(8,128)} %convolution_multiply_fusion.2), calls=%async_computation.5 | async-start | bytes 4194304 | tf_op jit(solution)/shard_map/all_to_all | solution.py:84
  321.3 6.5 %copy-start.4 = (f32[8192,256]{1,0:T(8,128)S(1)}, f32[8192,256]{1,0:T(8,128)}, u32[]{:S(2)}) copy-start(f32[8192,256]{1,0:T(8,128)} %copy.104) | copy-start | bytes 25165828
  332.5 7.6 %copy-start.11 = (f32[16,64,128]{2,0,1:T(8,128)S(1)}, f32[16,64,128]{2,0,1:T(8,128)}, u32[]{:S(2)}) copy-start(f32[16,64,128]{2,0,1:T(8,128)} %convolution_add_fusion.3) | copy-start | bytes 1572868
  343.6 0.8 copy-start.10
  344.4 80.3 %copy-start.8 = (f32[64,2048]{1,0:T(8,128)S(1)}, f32[64,2048]{1,0:T(8,128)}, u32[]{:S(2)}) copy-start(f32[64,2048]{1,0:T(8,128)} %copy-done.7) | copy-start | bytes 1572868
  427.1 27.3 %all-to-all-start.6 = ((bf16[16,4,64,128]{3,2,1,0:T(8,128)(2,1)}), bf16[16,4,64,128]{3,2,1,0:T(8,128)(2,1)}, u32[]{:S(2)}, u32[]{:S(2)}) async-start(bf16[16,4,64,128]{3,2,1,0:T(8,128)(2,1)} %bitcast.368), calls=%async_computation.6 | async-start | bytes 2097152 | tf_op jit(solution)/shard_map/all_to_all | solution.py:72
  454.4 86.7 %all-to-all-start.7 = ((f32[16,4,64,128]{3,2,1,0:T(8,128)}), f32[16,4,64,128]{3,2,1,0:T(8,128)}, u32[]{:S(2)}, u32[]{:S(2)}) async-start(f32[16,4,64,128]{3,2,1,0:T(8,128)} %convolution_multiply_fusion), calls=%async_computation.7 | async-start | bytes 4194304 | tf_op jit(solution)/shard_map/all_to_all | solution.py:84
  525.5 6.7 %copy-start.5 = (f32[8192,256]{1,0:T(8,128)S(1)}, f32[8192,256]{1,0:T(8,128)}, u32[]{:S(2)}) copy-start(f32[8192,256]{1,0:T(8,128)} %copy.112) | copy-start | bytes 25165828
  544.6 82.2 %copy-start.1 = (f32[64,2048]{1,0:T(8,128)S(1)}, f32[64,2048]{1,0:T(8,128)}, u32[]{:S(2)}) copy-start(f32[64,2048]{1,0:T(8,128)} %param.23) | copy-start | bytes 1572868
  625.0 1.8 copy-start.12
  625.4 1.4 copy-start.14
where the time goes:
time: 639 us; the launch traced here: 627 us
  blocking collectives  187 us (29%)
  local copies, waits for them, and re-layouts  154 us (24%)
  matrix products  148 us (23%)
  other arithmetic  48.4 us (8%)
  starting transfers between devices  46.6 us (7%)
  waiting for transfers between devices  40.8 us (6%)
    psum x3, blocking collectives, shards(): gram_sum, cross_sum = lax.psum((gram_part, cross_part), 'rows')  187 us
    unnamed x43, local copies, waits for them, and re-layouts  67.8 us
    dot_general x16, matrix products, add_blocks(): jnp.dot(selector, flat, precision=highest, preferred_element_type=jnp.flo...  55.5 us
    dot_general x6, local copies, waits for them, and re-layouts, add_blocks(): jnp.dot(selector, flat, precision=highest, preferred_element_type=jnp.flo...  55 us
    all_to_all x3, waiting for transfers between devices, shards(): lax.all_to_all(basis_bf[wanted_col], 'rows', split_axis=0, concat_axis=0,...  36 us
    dot_general x3, matrix products, shards(): jnp.einsum('tij,tkj->tki', local_tiles, basis_bf[local_col], preferred_el...  31.5 us
    dot_general x3, matrix products, shards(): jnp.einsum('tji,tkj->tki', local_tiles, basis_bf[local_row], preferred_el...  20.9 us
    all_to_all x3, starting transfers between devices, shards(): lax.all_to_all(returned, 'rows', split_axis=0, concat_axis=0, tiled=True)  20.3 us
  transfers between devices with their start and end apart: 8, of which 4 were waited for; matrix products, arithmetic and copies ran while one was open for 43% of the time, Pallas kernels for 0%

commit v1 on v0

v1 whole, which is shorter than its diff:
```python
import functools

import jax
import jax.numpy as jnp
from jax import lax
from jax.experimental import pallas as pl
from jax.experimental.pallas import tpu as pltpu
from jax.sharding import PartitionSpec as P

highest = lax.Precision.HIGHEST
f32 = jnp.float32
bf16 = jnp.bfloat16
NT = (((1,), (1,)), ((), ()))
MIB = 1024 * 1024


def dot_nt(a, b, precision=None):
    return lax.dot_general(a, b, NT, precision=precision, preferred_element_type=f32)


def dot_nn(a, b, precision=None):
    return jnp.dot(a, b, precision=precision, preferred_element_type=f32)


def fold(square):
    half = square.shape[0] // 2
    return jnp.concatenate([square[:half], square[half:]], axis=1)


def unfold(folded):
    half = folded.shape[1] // 2
    return jnp.concatenate([folded[:, :half], folded[:, half:]], axis=0)


def peer_barrier(me, size):
    barrier = pltpu.get_barrier_semaphore()
    for k in range(1, size):
        pl.semaphore_signal(
            barrier, inc=1, device_id={"rows": lax.rem(me + k, size)}, device_id_type=pl.DeviceIdType.MESH
        )
    pl.semaphore_wait(barrier, size - 1)


def ordered_sum(me, size, part_ref, buf):
    buf[0] = part_ref[...]
    total = buf[me]
    for p in range(1, size):
        total = total + buf[lax.rem(me - p + size, size)]
    return total


def remote(src, dst, send, recv, target):
    return pltpu.make_async_remote_copy(
        src_ref=src,
        dst_ref=dst,
        send_sem=send,
        recv_sem=recv,
        device_id={"rows": target},
        device_id_type=pl.DeviceIdType.MESH,
    )


def dense_kernel(per_step, count_ref, row_ref, col_ref, tiles_ref, dense_ref, acc):
    step = pl.program_id(0)
    edge = tiles_ref.shape[1]

    @pl.when(step == 0)
    def _():
        acc[...] = jnp.zeros_like(acc)

    for t in range(per_step):
        slot = step * per_step + t

        @pl.when(slot < count_ref[0])
        def _():
            r = pl.multiple_of(row_ref[slot] * edge, edge)
            c = pl.multiple_of(col_ref[slot] * edge, edge)
            acc[pl.ds(r, edge), pl.ds(c, edge)] += tiles_ref[t].astype(f32)

    @pl.when(step == pl.num_programs(0) - 1)
    def _():
        dense_ref[...] = acc[...].astype(bf16)


def dense_local(count, row, col, tiles, nodes):
    slots, edge, _ = tiles.shape
    per_step = 16
    return pl.pallas_call(
        functools.partial(dense_kernel, per_step),
        grid_spec=pltpu.PrefetchScalarGridSpec(
            num_scalar_prefetch=3,
            grid=(slots // per_step,),
            in_specs=[pl.BlockSpec((per_step, edge, edge), lambda i, *_: (i, 0, 0))],
            out_specs=pl.BlockSpec((nodes, nodes), lambda i, *_: (0, 0)),
            scratch_shapes=[pltpu.VMEM((nodes, nodes), f32)],
        ),
        out_shape=jax.ShapeDtypeStruct((nodes, nodes), bf16),
        compiler_params=pltpu.CompilerParams(vmem_limit_bytes=44 * MIB),
        cost_estimate=pl.CostEstimate(flops=10**9, bytes_accessed=40 * MIB, transcendentals=0),
        name="dense_local",
    )(count, row, col, tiles)


def gather_kernel(size, node_total, x_ref, gram_ref, xg_ref, inv_ref, gbuf, g_send, g_recv, own_send, own_sem,
                  z_recv, y_recv, s_recv, f_send, s_send):
    me = lax.axis_index("rows")
    deep = size // 4
    core = lax.rem(me, 2)
    mid = lax.rem(me // 2, 2)
    sib = me + 1 - 2 * core
    ynb = me + 2 - 4 * mid

    def back(base, k):
        return lax.rem(base - 4 * k + size, size)

    peer_barrier(me, size)
    waits = []
    small = []
    for k in range(1, size):
        copy = remote(gram_ref, gbuf.at[k], g_send.at[k], g_recv.at[k], lax.rem(me + k, size))
        copy.start()
        small.append(copy)
    copy = remote(x_ref, xg_ref.at[me], own_send.at[0], y_recv.at[0], ynb)
    copy.start()
    waits.append(copy)
    for k in range(1, deep):
        copy = remote(x_ref, xg_ref.at[me], own_send.at[k], z_recv.at[k], lax.rem(me + 4 * k, size))
        copy.start()
        waits.append(copy)
    copy = remote(x_ref, xg_ref.at[me], own_send.at[deep], s_recv.at[0], sib)
    copy.start()
    waits.append(copy)
    own = pltpu.make_async_copy(x_ref, xg_ref.at[me], own_sem)
    own.start()

    for k in range(1, deep):
        src = back(me, k)
        remote(x_ref, xg_ref.at[src], own_send.at[k], z_recv.at[k], ynb).wait_recv()
        copy = remote(xg_ref.at[src], xg_ref.at[src], f_send.at[k], y_recv.at[k], ynb)
        copy.start()
        waits.append(copy)
        copy = remote(xg_ref.at[src], xg_ref.at[src], s_send.at[k], s_recv.at[k], sib)
        copy.start()
        waits.append(copy)

    for copy in small:
        copy.wait_recv()
    gram = unfold(ordered_sum(me, size, gram_ref, gbuf)) / node_total
    n = gram.shape[0]
    rows = lax.broadcasted_iota(jnp.int32, (n, 2 * n), 0)
    lanes = lax.broadcasted_iota(jnp.int32, (n, 2 * n), 1)
    unit = jnp.where(rows == lanes, 1.0, 0.0)
    both = jnp.where(lanes < n, unit, jnp.concatenate([gram, gram], axis=1))

    def eliminate(k, both):
        row = jnp.sum(jnp.where(rows == k, both, 0.0), axis=0, keepdims=True)
        col = jnp.sum(jnp.where(lanes == k + n, both, 0.0), axis=1, keepdims=True)
        pivot = jnp.sum(jnp.where(lanes[:1] == k + n, row, 0.0), axis=1, keepdims=True)
        scaled = row * (1.0 / pivot)
        return both - jnp.where(rows > k, col * scaled, 0.0)

    both = lax.fori_loop(0, n, eliminate, both)
    diag = jnp.sum(jnp.where(lanes == rows + n, both, 0.0), axis=1, keepdims=True)
    inv_ref[...] = (both * (1.0 / jnp.sqrt(diag)))[:, :n]

    for k in range(deep):
        src = back(ynb, k)
        remote(x_ref, xg_ref.at[src], own_send.at[0], y_recv.at[k], ynb).wait_recv()
        copy = remote(xg_ref.at[src], xg_ref.at[src], s_send.at[deep + k], s_recv.at[deep + k], sib)
        copy.start()
        waits.append(copy)
    other = sib + 2 - 4 * mid
    for k in range(deep):
        src = back(sib, k)
        remote(x_ref, xg_ref.at[src], own_send.at[0], s_recv.at[k], sib).wait_recv()
    for k in range(deep):
        src = back(other, k)
        remote(x_ref, xg_ref.at[src], own_send.at[0], s_recv.at[deep + k], sib).wait_recv()
    for copy in small + waits:
        copy.wait_send()
    own.wait()


def gather_basis(x_bf, gram_part, size, node_total):
    columns, nodes = x_bf.shape
    deep = size // 4
    dma = pltpu.SemaphoreType.DMA
    return pl.pallas_call(
        functools.partial(gather_kernel, size, float(node_total)),
        in_specs=[pl.BlockSpec(memory_space=pl.ANY), pl.BlockSpec(memory_space=pltpu.VMEM)],
        out_specs=[pl.BlockSpec(memory_space=pl.ANY), pl.BlockSpec(memory_space=pltpu.VMEM)],
        out_shape=[
            jax.ShapeDtypeStruct((size, columns, nodes), bf16),
            jax.ShapeDtypeStruct((columns, columns), f32),
        ],
        scratch_shapes=[
            pltpu.VMEM((size,) + gram_part.shape, f32),
            dma((size,)),
            dma((size,)),
            dma((deep + 1,)),
            dma,
            dma((deep,)),
            dma((deep,)),
            dma((2 * deep,)),
            dma((deep,)),
            dma((2 * deep,)),
        ],
        compiler_params=pltpu.CompilerParams(
            collective_id=0, has_side_effects=True, vmem_limit_bytes=16 * MIB
        ),
        name="gather_basis",
    )(x_bf, gram_part)


def sum_kernel(size, part_ref, out_ref, buf, send, recv):
    me = lax.axis_index("rows")
    peer_barrier(me, size)
    copies = []
    for k in range(1, size):
        copy = remote(part_ref, buf.at[k], send.at[k], recv.at[k], lax.rem(me + k, size))
        copy.start()
        copies.append(copy)
    for copy in copies:
        copy.wait()
    out_ref[...] = ordered_sum(me, size, part_ref, buf)


def sum_rows(part, size):
    dma = pltpu.SemaphoreType.DMA
    return pl.pallas_call(
        functools.partial(sum_kernel, size),
        in_specs=[pl.BlockSpec(memory_space=pltpu.VMEM)],
        out_specs=pl.BlockSpec(memory_space=pltpu.VMEM),
        out_shape=jax.ShapeDtypeStruct(part.shape, f32),
        scratch_shapes=[pltpu.VMEM((size,) + part.shape, f32), dma((size,)), dma((size,))],
        compiler_params=pltpu.CompilerParams(
            collective_id=1, has_side_effects=True, vmem_limit_bytes=16 * MIB
        ),
        name="sum_rows",
    )(part)


def apply_kernel(first, slots, own_src, own_dst, in_src, in_dst, *refs):
    if first:
        dense_ref, own_ref, in_ref, xg_ref, x_ref, image_ref, cross_ref, degree_ref, acc, far = refs
    else:
        dense_ref, own_ref, in_ref, xg_ref, x_ref, degree_ref, image_ref, cross_ref, acc, far = refs
    step = pl.program_id(0)
    columns, nodes = x_ref.shape
    edge = own_ref.shape[1]
    chunk = dense_ref.shape[0]

    def with_ones(x):
        if first:
            return jnp.concatenate([x, jnp.ones((16, x.shape[1]), bf16)], axis=0)
        return x

    @pl.when(step == 0)
    def _():
        acc[...] = jnp.zeros_like(acc)
        far[...] = jnp.zeros_like(far)

    x_all = with_ones(x_ref[...].astype(bf16))
    here = pl.ds(pl.multiple_of(step * chunk, chunk), chunk)
    x_here = with_ones(x_ref[:, here].astype(bf16))
    dense = dense_ref[...]
    acc[...] += dot_nn(x_here, dense)
    acc[:, here] += dot_nt(x_all, dense)

    count = own_ref.shape[0]
    blocks = nodes // edge
    for tiles_ref, src_ref, dst_ref, dot in (
        (own_ref, own_src, own_dst, dot_nt),
        (in_ref, in_src, in_dst, dot_nn),
    ):
        products = []
        for t in range(count):
            slot = step * count + t
            at = pl.ds(pl.multiple_of(src_ref[slot] * edge, edge), edge)
            products.append(dot(with_ones(xg_ref[slot // slots, :, at]), tiles_ref[t]))
        for t in range(count):
            far[dst_ref[step * count + t]] += products[t]

    @pl.when(step == pl.num_programs(0) - 1)
    def _():
        for b in range(blocks):
            at = slice(b * edge, (b + 1) * edge)
            both = acc[:, at] + far[b]
            if first:
                degree = 0.5 * both[columns : columns + 1]
                degree_ref[:, at] = jnp.broadcast_to(degree, (8, edge))
            else:
                degree = degree_ref[:1, at]
            image_ref[:, at] = degree * x_ref[:, at] - 0.5 * both[:columns]
        cross_ref[...] = fold(dot_nt(image_ref[...], x_ref[...], highest))


def apply_operator(first, slots, index, dense, own_tiles, in_tiles, xg, x, degree):
    columns, nodes = x.shape
    edge = own_tiles.shape[1]
    steps = 8
    chunk = nodes // steps
    count = own_tiles.shape[0] // steps
    whole = lambda shape: pl.BlockSpec(shape, lambda i, *_: (0,) * len(shape))
    rows = columns + 16 if first else columns
    tile_spec = pl.BlockSpec((count, edge, edge), lambda i, *_: (i, 0, 0))
    degree_shape = (8, nodes)
    in_specs = [
        pl.BlockSpec((chunk, nodes), lambda i, *_: (i, 0)),
        tile_spec,
        tile_spec,
        whole(xg.shape),
        whole(x.shape),
    ]
    out_specs = [whole(x.shape), whole((columns // 2, 2 * columns))]
    out_shape = [
        jax.ShapeDtypeStruct(x.shape, f32),
        jax.ShapeDtypeStruct((columns // 2, 2 * columns), f32),
    ]
    operands = [dense, own_tiles, in_tiles, xg, x]
    if first:
        out_specs.append(whole(degree_shape))
        out_shape.append(jax.ShapeDtypeStruct(degree_shape, f32))
    else:
        in_specs.append(whole(degree_shape))
        operands.append(degree)
    return pl.pallas_call(
        functools.partial(apply_kernel, first, slots),
        grid_spec=pltpu.PrefetchScalarGridSpec(
            num_scalar_prefetch=4,
            grid=(steps,),
            in_specs=in_specs,
            out_specs=out_specs,
            scratch_shapes=[
                pltpu.VMEM((rows, nodes), f32),
                pltpu.VMEM((nodes // edge + 1, rows, edge), f32),
            ],
        ),
        out_shape=out_shape,
        compiler_params=pltpu.CompilerParams(vmem_limit_bytes=44 * MIB),
        name="apply_operator",
    )(*index, *operands)


def update_kernel(last, node_total, inv_ref, cross_ref, image_ref, x_ref, degree_ref, *refs):
    inv = inv_ref[...]
    n = inv.shape[0]
    cross = unfold(cross_ref[...]) / node_total
    projected = dot_nt(dot_nn(inv, cross, highest), inv, highest)
    scale = 1.0 / (1.0 + degree_ref[:1, :])
    x = x_ref[...]
    p_inv = dot_nn(projected, inv, highest)
    if last:
        ortho_ref, residual_ref, projected_ref = refs
        ortho_ref[...] = dot_nn(inv, x, highest)
        residual_ref[...] = (dot_nn(inv, image_ref[...], highest) - dot_nn(p_inv, x, highest)) * scale
        projected_ref[...] = projected
    else:
        coeff_ref, dir_ref, x_out, bf_out, dir_out, gram_out = refs
        c_x, c_r, c_p = coeff_ref[:, :n], coeff_ref[:, n : 2 * n], coeff_ref[:, 2 * n :]
        m_image = dot_nn(c_r, inv, highest)
        m_x = dot_nn(c_r, p_inv, highest)
        m_basis = dot_nn(c_x, inv, highest)
        direction = (dot_nn(m_image, image_ref[...], highest) - dot_nn(m_x, x, highest)) * scale
        direction = direction + dot_nn(c_p, dir_ref[...], highest)
        basis = dot_nn(m_basis, x, highest) + direction
        dir_out[...] = direction
        x_out[...] = basis
        bf_out[...] = basis.astype(bf16)
        gram_out[...] = fold(dot_nt(basis, basis, highest))


def update(last, node_total, inv, cross, image, x, degree, coeff=None, direction=None):
    columns, nodes = x.shape
    big = jax.ShapeDtypeStruct((columns, nodes), f32)
    if last:
        shapes = [big, big, jax.ShapeDtypeStruct((columns, columns), f32)]
        operands = (inv, cross, image, x, degree)
    else:
        shapes = [
            big,
            jax.ShapeDtypeStruct((columns, nodes), bf16),
            big,
            jax.ShapeDtypeStruct((columns // 2, 2 * columns), f32),
        ]
        operands = (inv, cross, image, x, degree, coeff, direction)
    vmem = pl.BlockSpec(memory_space=pltpu.VMEM)
    return pl.pallas_call(
        functools.partial(update_kernel, last, float(node_total)),
        in_specs=[vmem] * len(operands),
        out_specs=[vmem] * len(shapes),
        out_shape=shapes,
        compiler_params=pltpu.CompilerParams(vmem_limit_bytes=32 * MIB),
        name="update",
    )(*operands)


def start_kernel(x_ref, bf_out, gram_out):
    x = x_ref[...]
    bf_out[...] = x.astype(bf16)
    gram_out[...] = fold(dot_nt(x, x, highest))


def start(x):
    columns, nodes = x.shape
    vmem = pl.BlockSpec(memory_space=pltpu.VMEM)
    return pl.pallas_call(
        start_kernel,
        in_specs=[vmem],
        out_specs=[vmem] * 2,
        out_shape=[
            jax.ShapeDtypeStruct((columns, nodes), bf16),
            jax.ShapeDtypeStruct((columns // 2, 2 * columns), f32),
        ],
        compiler_params=pltpu.CompilerParams(vmem_limit_bytes=16 * MIB),
        name="start",
    )(x)


def shards(
    local_tiles,
    local_row,
    local_col,
    local_count,
    remote_tiles,
    remote_row,
    remote_col,
    remote_count,
    start_basis,
    start_dir,
    coeffs,
):
    size = lax.axis_size("rows")
    edge = local_tiles.shape[1]
    columns, nodes = start_basis.shape
    blocks = nodes // edge
    slots = remote_tiles.shape[1]
    node_total = nodes * size
    live = jnp.arange(slots)[None, :] < remote_count[:, None]
    packed = remote_row + blocks * jnp.where(live, remote_col, blocks)
    far_packed = lax.all_to_all(packed, "rows", split_axis=0, concat_axis=0, tiled=True).reshape(-1)
    in_tiles = lax.all_to_all(remote_tiles, "rows", split_axis=0, concat_axis=0, tiled=True)
    in_tiles = in_tiles.reshape(-1, edge, edge)
    own_tiles = remote_tiles.reshape(-1, edge, edge)
    own_dst = jnp.where(live, remote_row, blocks).reshape(-1)
    index = (remote_col.reshape(-1), own_dst, far_packed % blocks, far_packed // blocks)
    dense = dense_local(local_count, local_row, local_col, local_tiles, nodes)
    basis = start_basis
    direction = start_dir
    degree = None
    basis_bf, gram_part = start(basis)
    passes = coeffs.shape[0]
    for iteration in range(passes + 1):
        xg, inv = gather_basis(basis_bf, gram_part, size, node_total)
        out = apply_operator(iteration == 0, slots, index, dense, own_tiles, in_tiles, xg, basis, degree)
        image, cross_part = out[:2]
        if iteration == 0:
            degree = out[2]
        cross = sum_rows(cross_part, size)
        if iteration < passes:
            basis, basis_bf, direction, gram_part = update(
                False, node_total, inv, cross, image, basis, degree, coeffs[iteration], direction
            )
    return update(True, node_total, inv, cross, image, basis, degree)


def solution(mesh):
    placed = (
        P(("groups", "rows"), None, None),
        P(("groups", "rows")),
        P(("groups", "rows")),
        P(("groups", "rows")),
        P(("groups", "rows"), None, None, None),
        P(("groups", "rows"), None),
        P(("groups", "rows"), None),
        P(("groups", "rows")),
        P("groups", "rows"),
        P("groups", "rows"),
        P("groups", None, None),
    )
    return jax.shard_map(
        shards,
        mesh=mesh,
        in_specs=placed,
        out_specs=(P("groups", "rows"), P("groups", "rows"), P("groups", None)),
        check_vma=False,
    )
```

time: 639 us -> 301 us (0.47); the launches traced: 627 us -> 300 us
  Pallas kernels: 0 us -> 270 us
  blocking collectives: 187 us -> 13.6 us
  matrix products: 148 us -> 0 us
  local copies, waits for them, and re-layouts: 154 us -> 8.44 us
  other arithmetic: 48.4 us -> 1.44 us
  starting transfers between devices: 46.6 us -> 4.45 us
  waiting for transfers between devices: 40.8 us -> 0.01 us
    pallas_call x0 -> x14, Pallas kernels: none -> 270 us  [the longest x3 172 us: gather_basis(): pl.pallas_call(functools.partial(gather_kernel, size, float(node_total)),...]
    psum x3 -> x0, blocking collectives: 187 us -> none  [shards(): gram_sum, cross_sum = lax.psum((gram_part, cross_part), 'rows')]
    dot_general x55 -> x0, matrix products: 147 us -> none  [the longest x16 55.5 us: add_blocks(): jnp.dot(selector, flat, precision=highest, preferred_element_type=jnp.flo...]
    unnamed x43 -> x21, local copies, waits for them, and re-layouts: 67.8 us -> 7.49 us
    dot_general x6 -> x0, local copies, waits for them, and re-layouts: 55 us -> none  [add_blocks(): jnp.dot(selector, flat, precision=highest, preferred_element_type=jnp.flo...]
    all_to_all x8 -> x1, starting transfers between devices: 46.6 us -> 4.45 us  [shards(): lax.all_to_all(remote_tiles, 'rows', split_axis=0, concat_axis=0, tiled=T...]
    all_to_all x8 -> x1, waiting for transfers between devices: 40.8 us -> 0.01 us  [shards(): lax.all_to_all(remote_tiles, 'rows', split_axis=0, concat_axis=0, tiled=T...]
    another operation x15 -> x0, other arithmetic: 36.2 us -> none  [the longest x9 19.6 us: shards(): lower_chol = jnp.linalg.cholesky(gram_now)]
  transfers between devices with their start and end apart: 8 -> 1, of which waited for: 4 -> 0; matrix products, arithmetic and copies ran while one was open for 43% -> 1% of each run, Pallas kernels for 0% -> 33%
where the time goes in v1:
time: 301 us; the launch traced here: 300 us
  Pallas kernels  270 us (90%)
  blocking collectives  13.6 us (5%)
  local copies, waits for them, and re-layouts  8.44 us (3%)
  starting transfers between devices  4.45 us (1%)
    pallas_call x3, Pallas kernels, gather_basis(): pl.pallas_call(functools.partial(gather_kernel, size, float(node_total)),...  172 us
    pallas_call x3, Pallas kernels, sum_rows(): pl.pallas_call(functools.partial(sum_kernel, size), in_specs=[pl.BlockSpe...  40.7 us
    pallas_call x3, Pallas kernels, apply_operator(): pl.pallas_call(functools.partial(apply_kernel, first, slots), grid_spec=p...  33.2 us
    all_to_all x1, blocking collectives, shards(): lax.all_to_all(packed, 'rows', split_axis=0, concat_axis=0, tiled=True)  13.6 us
    pallas_call x1, Pallas kernels, dense_local(): pl.pallas_call(functools.partial(dense_kernel, per_step), grid_spec=pltpu...  13.5 us
    pallas_call x3, Pallas kernels, update(): pl.pallas_call(functools.partial(update_kernel, last, float(node_total)),...  9.68 us
    unnamed x21, local copies, waits for them, and re-layouts  7.49 us
  transfers between devices with their start and end apart: 1, of which 0 were waited for; matrix products, arithmetic and copies ran while one was open for 1% of the time, Pallas kernels for 33%

profile of v1, /device:TPU:0, one launch (start us, length us, event | category | flops | bytes accessed | tf_op | source)
XLA Modules:
  0.0 299.6 jit_solution(11149154062077642359)
XLA Ops:
  0.6 0.0 copy-start.9
  0.6 0.0 copy-start.2
  0.7 0.0 copy-start.7
  0.7 0.8 add_bitcast_fusion
  1.4 0.1 copy.22
  1.5 13.6 %all_to_all.14 = s32[16,1,4]{2,1,0:T(1,128)S(1)} all-to-all(s32[16,1,4]{2,1,0:T(1,128)S(1)} %copy.22), channel_id=1, replica_groups=mesh['groups'=2,'rows'=16] {'rows'}, dimensions={0} | all-to-all | bytes 512 | tf_op jit(solution)/shard_map/all_to_all | solution.py:441
  15.1 4.5 %all-to-all-start.1 = ((bf16[16,4,128,128]{3,2,1,0:T(8,128)(2,1)}), bf16[16,4,128,128]{3,2,1,0:T(8,128)(2,1)}, u32[]{:S(2)}, u32[]{:S(2)}) async-start(bf16[16,4,128,128]{3,2,1,0:T(8,128)(2,1)} %param.15), calls=%async_computation.1 | async-start | bytes 4194304 | tf_op jit(solution)/shard_map/all_to_all | solution.py:442
  19.6 0.1 copy.20
  20.3 0.1 copy.21
  20.4 0.1 reshape.26.own_dst
  20.5 0.1 reshape.25.own_src
  20.6 0.6 start.1
  21.2 84.9 %gather_basis.3 = (bf16[16,64,2048]{2,1,0:T(8,128)(2,1)S(1)}, f32[64,64]{1,0:T(8,128)S(1)}) custom-call(bf16[64,2048]{1,0:T(8,128)(2,1)S(1)} %get-tuple-element.25.x_ref, f32[32,128]{1,0:T(8,128)S(1)} %get-tuple-element.26.gram_ref), custom_call_target="tpu_custom_call" | custom-call | tf_op jit(solution)/shard_map/gather_basis/pallas_call | solution.py:188
  106.1 2.0 copy-done.3
  108.1 13.5 %dense_local.1.refs_0_ = bf16[2048,2048]{1,0:T(8,128)(2,1)S(1)} custom-call(s32[1]{0:T(128)S(6)} %copy.23.count_ref, s32[256]{0:T(256)S(1)} %copy-done.6, s32[256]{0:T(256)S(1)} %copy-done.7, bf16[256,128,128]{2,1,0:T(8,128)(2,1)} %tiles_ref.1), custom_call_target="tpu_custom_call" | custom-call | flops 1000000000 | bytes 41943040 | tf_op jit(solution)/shard_map/dense_local/pallas_call | solution.py:88
  121.6 3.2 %copy-done = bf16[2048,2048]{1,0:T(8,128)(2,1)} copy-done((bf16[2048,2048]{1,0:T(8,128)(2,1)}, bf16[2048,2048]{1,0:T(8,128)(2,1)S(1)}, u32[]{:S(2)}) %copy-start) | copy-done | bytes 8388632
  124.9 0.5 broadcast.28
  125.4 0.7 reduce.3
  126.1 0.1 reshape.27
  126.2 0.0 all-to-all-done.1
  126.2 2.2 copy-done.4
  128.4 11.1 %apply_operator.3 = (f32[64,2048]{1,0:T(8,128)S(1)}, f32[32,128]{1,0:T(8,128)S(1)}, f32[8,2048]{1,0:T(8,128)S(1)}) custom-call(s32[64]{0:T(128)S(1)} %reshape.25.own_src, s32[64]{0:T(128)S(1)} %reshape.26.own_dst, s32[64]{0:T(128)S(1)} %get-tuple-element.52.in_src, s32[64]{0:T(128)S(1)} %get-tuple-element.51.in_dst, bf16[2048,2048]{1,0:T(8,128)(2,1)} %copy-done, ...), custom_call_target="tpu_custom_call" | custom-call | tf_op jit(solution)/shard_map/apply_operator/pallas_call | solution.py:327
  139.5 13.3 %sum_rows.3.cross_ref = f32[32,128]{1,0:T(8,128)S(1)} custom-call(f32[32,128]{1,0:T(8,128)S(1)} %get-tuple-element.29.part_ref), custom_call_target="tpu_custom_call" | custom-call | tf_op jit(solution)/shard_map/sum_rows/pallas_call | solution.py:230
  152.8 3.2 %update.3 = (f32[64,2048]{1,0:T(8,128)S(1)}, bf16[64,2048]{1,0:T(8,128)(2,1)S(1)}, f32[64,2048]{1,0:T(8,128)S(1)}, f32[32,128]{1,0:T(8,128)S(1)}) custom-call(f32[64,64]{1,0:T(8,128)S(1)} %get-tuple-element.27.inv_ref, f32[32,128]{1,0:T(8,128)S(1)} %sum_rows.3.cross_ref, f32[64,2048]{1,0:T(8,128)S(1)} %get-tuple-element.30.image_ref, ...), custom_call_target="tpu_custom_call" | custom-call | tf_op jit(solution)/shard_map/update/pallas_call | solution.py:388
  156.1 43.7 %gather_basis.4 = (bf16[16,64,2048]{2,1,0:T(8,128)(2,1)S(1)}, f32[64,64]{1,0:T(8,128)S(1)}) custom-call(bf16[64,2048]{1,0:T(8,128)(2,1)S(1)} %get-tuple-element.32.x_ref, f32[32,128]{1,0:T(8,128)S(1)} %get-tuple-element.33.gram_ref), custom_call_target="tpu_custom_call" | custom-call | tf_op jit(solution)/shard_map/gather_basis/pallas_call | solution.py:188
  199.8 11.1 %apply_operator.4 = (f32[64,2048]{1,0:T(8,128)S(1)}, f32[32,128]{1,0:T(8,128)S(1)}) custom-call(s32[64]{0:T(128)S(1)} %reshape.25.own_src, s32[64]{0:T(128)S(1)} %reshape.26.own_dst, s32[64]{0:T(128)S(1)} %get-tuple-element.52.in_src, s32[64]{0:T(128)S(1)} %get-tuple-element.51.in_dst, bf16[2048,2048]{1,0:T(8,128)(2,1)} %copy-done, ...), custom_call_target="tpu_custom_call" | custom-call | tf_op jit(solution)/shard_map/apply_operator/pallas_call | solution.py:327
  210.9 13.6 %sum_rows.4.cross_ref = f32[32,128]{1,0:T(8,128)S(1)} custom-call(f32[32,128]{1,0:T(8,128)S(1)} %get-tuple-element.37.part_ref), custom_call_target="tpu_custom_call" | custom-call | tf_op jit(solution)/shard_map/sum_rows/pallas_call | solution.py:230
  224.6 3.8 %update.4 = (f32[64,2048]{1,0:T(8,128)S(1)}, bf16[64,2048]{1,0:T(8,128)(2,1)S(1)}, f32[64,2048]{1,0:T(8,128)}, f32[32,128]{1,0:T(8,128)S(1)}) custom-call(f32[64,64]{1,0:T(8,128)S(1)} %get-tuple-element.34.inv_ref, f32[32,128]{1,0:T(8,128)S(1)} %sum_rows.4.cross_ref, f32[64,2048]{1,0:T(8,128)S(1)} %get-tuple-element.38.image_ref, ...), custom_call_target="tpu_custom_call" | custom-call | tf_op jit(solution)/shard_map/update/pallas_call | solution.py:388
  228.4 43.9 %gather_basis.5 = (bf16[16,64,2048]{2,1,0:T(8,128)(2,1)S(1)}, f32[64,64]{1,0:T(8,128)S(1)}) custom-call(bf16[64,2048]{1,0:T(8,128)(2,1)S(1)} %get-tuple-element.40.x_ref, f32[32,128]{1,0:T(8,128)S(1)} %get-tuple-element.41.gram_ref), custom_call_target="tpu_custom_call" | custom-call | tf_op jit(solution)/shard_map/gather_basis/pallas_call | solution.py:188
  272.2 11.0 %apply_operator.5 = (f32[64,2048]{1,0:T(8,128)S(1)}, f32[32,128]{1,0:T(8,128)S(1)}) custom-call(s32[64]{0:T(128)S(1)} %reshape.25.own_src, s32[64]{0:T(128)S(1)} %reshape.26.own_dst, s32[64]{0:T(128)S(1)} %get-tuple-element.52.in_src, s32[64]{0:T(128)S(1)} %get-tuple-element.51.in_dst, bf16[2048,2048]{1,0:T(8,128)(2,1)} %copy-done, ...), custom_call_target="tpu_custom_call" | custom-call | tf_op jit(solution)/shard_map/apply_operator/pallas_call | solution.py:327
  283.2 13.8 %sum_rows.5.cross_ref = f32[32,128]{1,0:T(8,128)S(1)} custom-call(f32[32,128]{1,0:T(8,128)S(1)} %get-tuple-element.45.part_ref), custom_call_target="tpu_custom_call" | custom-call | tf_op jit(solution)/shard_map/sum_rows/pallas_call | solution.py:230
  297.0 2.6 update.5
  (16 shorter events, 0.0 us)
Async XLA Ops:
  0.6 18.9 %copy-start.9 = (s32[16,4]{0,1:T(4,128)S(1)}, s32[16,4]{0,1:T(4,128)}, u32[]{:S(2)}) copy-start(s32[16,4]{0,1:T(4,128)} %param.17) | copy-start | bytes 772
  0.6 19.9 %copy-start.2 = (f32[64,2048]{1,0:T(8,128)S(1)}, f32[64,2048]{1,0:T(8,128)}, u32[]{:S(2)}) copy-start(f32[64,2048]{1,0:T(8,128)} %x_ref.3) | copy-start | bytes 1572868
  0.7 107.4 %copy-start.7 = (s32[256]{0:T(256)S(1)}, s32[256]{0:T(256)}, u32[]{:S(2)}) copy-start(s32[256]{0:T(256)} %col_ref.1) | copy-start | bytes 3076
  0.7 107.4 %copy-start.6 = (s32[256]{0:T(256)S(1)}, s32[256]{0:T(256)}, u32[]{:S(2)}) copy-start(s32[256]{0:T(256)} %row_ref.1) | copy-start | bytes 3076
  15.1 111.1 %all-to-all-start.1 = ((bf16[16,4,128,128]{3,2,1,0:T(8,128)(2,1)}), bf16[16,4,128,128]{3,2,1,0:T(8,128)(2,1)}, u32[]{:S(2)}, u32[]{:S(2)}) async-start(bf16[16,4,128,128]{3,2,1,0:T(8,128)(2,1)} %param.15), calls=%async_computation.1 | async-start | bytes 4194304 | tf_op jit(solution)/shard_map/all_to_all | solution.py:442
  106.1 2.0 copy-start.3
  108.1 16.8 %copy-start.8 = (f32[2,64,192]{2,1,0:T(8,128)S(1)}, f32[2,64,192]{2,1,0:T(8,128)}, u32[]{:S(2)}) copy-start(f32[2,64,192]{2,1,0:T(8,128)} %param.21) | copy-start | bytes 294916
  108.1 18.1 %copy-start.1 = (bf16[16,4,128,128]{3,2,1,0:T(8,128)(2,1)S(1)}, bf16[16,4,128,128]{3,2,1,0:T(8,128)(2,1)}, u32[]{:S(2)}) copy-start(bf16[16,4,128,128]{3,2,1,0:T(8,128)(2,1)} %param.15) | copy-start | bytes 6291460
  121.6 3.2 %copy-start = (bf16[2048,2048]{1,0:T(8,128)(2,1)}, bf16[2048,2048]{1,0:T(8,128)(2,1)S(1)}, u32[]{:S(2)}) copy-start(bf16[2048,2048]{1,0:T(8,128)(2,1)S(1)} %dense_local.1.refs_0_) | copy-start | bytes 25165828
  126.2 2.2 copy-start.4
  128.4 24.4 %copy-start.5 = (f32[64,2048]{1,0:T(8,128)S(1)}, f32[64,2048]{1,0:T(8,128)}, u32[]{:S(2)}) copy-start(f32[64,2048]{1,0:T(8,128)} %refs_1_.1) | copy-start | bytes 1572868

commit v2 on v1

--- a/solution.py
+++ b/solution.py
@@ -32,20 +32,36 @@
     return jnp.concatenate([folded[:, :half], folded[:, half:]], axis=0)
 
 
-def peer_barrier(me, size):
+def peer_barrier(targets):
     barrier = pltpu.get_barrier_semaphore()
-    for k in range(1, size):
-        pl.semaphore_signal(
-            barrier, inc=1, device_id={"rows": lax.rem(me + k, size)}, device_id_type=pl.DeviceIdType.MESH
-        )
-    pl.semaphore_wait(barrier, size - 1)
-
-
-def ordered_sum(me, size, part_ref, buf):
+    for target in targets:
+        pl.semaphore_signal(barrier, inc=1, device_id={"rows": target}, device_id_type=pl.DeviceIdType.MESH)
+    pl.semaphore_wait(barrier, len(targets))
+
+
+def plane_peers(me):
+    base = me - lax.rem(me, 4)
+    return [base + lax.rem(me + k, 4) for k in range(1, 4)]
+
+
+def line_peers(me, size):
+    return [lax.rem(me + 4 * k, size) for k in range(1, size // 4)]
+
+
+def send_parts(part_ref, buf, send, recv, targets):
+    copies = []
+    for k, target in enumerate(targets):
+        copy = remote(part_ref, buf.at[k + 1], send.at[k], recv.at[k], target)
+        copy.start()
+        copies.append(copy)
+    return copies
+
+
+def ordered_sum(place, count, part_ref, buf):
     buf[0] = part_ref[...]
-    total = buf[me]
-    for p in range(1, size):
-        total = total + buf[lax.rem(me - p + size, size)]
+    total = buf[place]
+    for p in range(1, count):
+        total = total + buf[lax.rem(place - p + count, count)]
     return total
 
 
@@ -101,56 +117,9 @@
     )(count, row, col, tiles)
 
 
-def gather_kernel(size, node_total, x_ref, gram_ref, xg_ref, inv_ref, gbuf, g_send, g_recv, own_send, own_sem,
-                  z_recv, y_recv, s_recv, f_send, s_send):
-    me = lax.axis_index("rows")
-    deep = size // 4
-    core = lax.rem(me, 2)
-    mid = lax.rem(me // 2, 2)
-    sib = me + 1 - 2 * core
-    ynb = me + 2 - 4 * mid
-
-    def back(base, k):
-        return lax.rem(base - 4 * k + size, size)
-
-    peer_barrier(me, size)
-    waits = []
-    small = []
-    for k in range(1, size):
-        copy = remote(gram_ref, gbuf.at[k], g_send.at[k], g_recv.at[k], lax.rem(me + k, size))
-        copy.start()
-        small.append(copy)
-    copy = remote(x_ref, xg_ref.at[me], own_send.at[0], y_recv.at[0], ynb)
-    copy.start()
-    waits.append(copy)
-    for k in range(1, deep):
-        copy = remote(x_ref, xg_ref.at[me], own_send.at[k], z_recv.at[k], lax.rem(me + 4 * k, size))
-        copy.start()
-        waits.append(copy)
-    copy = remote(x_ref, xg_ref.at[me], own_send.at[deep], s_recv.at[0], sib)
-    copy.start()
-    waits.append(copy)
-    own = pltpu.make_async_copy(x_ref, xg_ref.at[me], own_sem)
-    own.start()
-
-    for k in range(1, deep):
-        src = back(me, k)
-        remote(x_ref, xg_ref.at[src], own_send.at[k], z_recv.at[k], ynb).wait_recv()
-        copy = remote(xg_ref.at[src], xg_ref.at[src], f_send.at[k], y_recv.at[k], ynb)
-        copy.start()
-        waits.append(copy)
-        copy = remote(xg_ref.at[src], xg_ref.at[src], s_send.at[k], s_recv.at[k], sib)
-        copy.start()
-        waits.append(copy)
-
-    for copy in small:
-        copy.wait_recv()
-    gram = unfold(ordered_sum(me, size, gram_ref, gbuf)) / node_total
-    n = gram.shape[0]
+def back_substitute(n, first, last, both):
     rows = lax.broadcasted_iota(jnp.int32, (n, 2 * n), 0)
     lanes = lax.broadcasted_iota(jnp.int32, (n, 2 * n), 1)
-    unit = jnp.where(rows == lanes, 1.0, 0.0)
-    both = jnp.where(lanes < n, unit, jnp.concatenate([gram, gram], axis=1))
 
     def eliminate(k, both):
         row = jnp.sum(jnp.where(rows == k, both, 0.0), axis=0, keepdims=True)
@@ -159,25 +128,121 @@
         scaled = row * (1.0 / pivot)
         return both - jnp.where(rows > k, col * scaled, 0.0)
 
-    both = lax.fori_loop(0, n, eliminate, both)
+    return lax.fori_loop(first, last, eliminate, both)
+
+
+def gather_kernel(size, node_total, x_ref, gram_ref, xg_ref, inv_ref, plane_buf, line_buf, half_sum, p_send, p_recv,
+                  l_send, l_recv, own_sem, z_send, z_recv, y_send, y_recv, s_send, s_recv):
+    me = lax.axis_index("rows")
+    deep = size // 4
+    z = me // 4
+    core = lax.rem(me, 2)
+    mid = lax.rem(me // 2, 2)
+    sib = me + 1 - 2 * core
+    ynb = me + 2 - 4 * mid
+    other = sib + 2 - 4 * mid
+    up, down = lax.rem(me + 4, size), lax.rem(me - 4 + size, size)
+    pieces = 2
+    piece = x_ref.shape[0] // pieces
+
+    def part(block, h):
+        return xg_ref.at[block, pl.ds(h * piece, piece)]
+
+    def along(base, k):
+        return lax.rem(base + 4 * k + size, size)
+
+    planes, lines = plane_peers(me), line_peers(me, size)
+    peer_barrier(planes + lines)
+    plane_copies = send_parts(gram_ref, plane_buf, p_send, p_recv, planes)
+
+    def hop(way, k, h):
+        return z_recv.at[way, k, h]
+
+    sends = []
+
+    def send(cond, copy):
+        if cond is None:
+            copy.start()
+        else:
+            pl.when(cond)(copy.start)
+        sends.append((cond, copy))
+
+    for h in range(pieces):
+        src = x_ref.at[pl.ds(h * piece, piece)]
+        send(None, remote(src, part(me, h), y_send.at[z, h], y_recv.at[z, h], ynb))
+        send(z + 1 < deep, remote(src, part(me, h), z_send.at[0, 0, h], hop(0, 1, h), up))
+        send(z > 0, remote(src, part(me, h), z_send.at[1, 0, h], hop(1, 1, h), down))
+        send(None, remote(src, part(me, h), s_send.at[0, z, h], s_recv.at[0, z, h], sib))
+    own = pltpu.make_async_copy(x_ref, xg_ref.at[me], own_sem)
+    own.start()
+
+    for copy in plane_copies:
+        copy.wait()
+    half_sum[...] = ordered_sum(lax.rem(me, 4), 4, gram_ref, plane_buf)
+    line_copies = send_parts(half_sum, line_buf, l_send, l_recv, lines)
+
+    def take_along_z(k):
+        for h in range(pieces):
+            for way, there, more, onto in (
+                (0, z >= k, z + 1 < deep, up),
+                (1, z + k < deep, z > 0, down),
+            ):
+                offset = -k if way == 0 else k
+                block = along(me, offset)
+                at = lax.rem(z + offset + deep, deep)
+                got = part(block, h)
+                pl.when(there)(remote(got, got, z_send.at[way, k, h], hop(way, k, h), onto).wait_recv)
+                send(there, remote(got, got, y_send.at[at, h], y_recv.at[at, h], ynb))
+                if k + 1 < deep:
+                    send(
+                        there & more,
+                        remote(got, got, z_send.at[way, k, h], hop(way, k + 1, h), onto),
+                    )
+                send(there, remote(got, got, s_send.at[0, at, h], s_recv.at[0, at, h], sib))
+
+    def take_along_y(k):
+        for h in range(pieces):
+            for offset, there in ((0, None),) if k == 0 else ((-k, z >= k), (k, z + k < deep)):
+                block = along(ynb, offset)
+                at = lax.rem(z + offset + deep, deep)
+                got = part(block, h)
+                wait = remote(got, got, y_send.at[at, h], y_recv.at[at, h], ynb).wait_recv
+                if there is None:
+                    wait()
+                else:
+                    pl.when(there)(wait)
+                send(there, remote(got, got, s_send.at[1, at, h], s_recv.at[1, at, h], sib))
+
+    n = inv_ref.shape[0]
+    rows = lax.broadcasted_iota(jnp.int32, (n, 2 * n), 0)
+    lanes = lax.broadcasted_iota(jnp.int32, (n, 2 * n), 1)
+    take_along_z(1)
+    for copy in line_copies:
+        copy.wait()
+    gram = unfold(ordered_sum(z, deep, half_sum, line_buf)) / node_total
+    unit = jnp.where(rows == lanes, 1.0, 0.0)
+    both = jnp.where(lanes < n, unit, jnp.concatenate([gram, gram], axis=1))
+    cut = [n * k // deep for k in range(deep + 1)]
+    for k in range(1, deep):
+        both = back_substitute(n, cut[k - 1], cut[k], both)
+        take_along_y(k - 1)
+        if k + 1 < deep:
+            take_along_z(k + 1)
+    both = back_substitute(n, cut[deep - 1], cut[deep], both)
+    take_along_y(deep - 1)
     diag = jnp.sum(jnp.where(lanes == rows + n, both, 0.0), axis=1, keepdims=True)
     inv_ref[...] = (both * (1.0 / jnp.sqrt(diag)))[:, :n]
 
-    for k in range(deep):
-        src = back(ynb, k)
-        remote(x_ref, xg_ref.at[src], own_send.at[0], y_recv.at[k], ynb).wait_recv()
-        copy = remote(xg_ref.at[src], xg_ref.at[src], s_send.at[deep + k], s_recv.at[deep + k], sib)
-        copy.start()
-        waits.append(copy)
-    other = sib + 2 - 4 * mid
-    for k in range(deep):
-        src = back(sib, k)
-        remote(x_ref, xg_ref.at[src], own_send.at[0], s_recv.at[k], sib).wait_recv()
-    for k in range(deep):
-        src = back(other, k)
-        remote(x_ref, xg_ref.at[src], own_send.at[0], s_recv.at[deep + k], sib).wait_recv()
-    for copy in small + waits:
-        copy.wait_send()
+    for at in range(deep):
+        for h in range(pieces):
+            for line, base in ((0, sib), (1, other)):
+                got = part(lax.rem(base, 4) + 4 * at, h)
+                remote(got, got, s_send.at[line, at, h], s_recv.at[line, at, h], sib).wait_recv()
+    for cond, copy in sends:
+        if cond is None:
+            copy.wait_send()
+        else:
+            pl.when(cond)(copy.wait_send)
     own.wait()
 
 
@@ -194,16 +259,20 @@
             jax.ShapeDtypeStruct((columns, columns), f32),
         ],
         scratch_shapes=[
-            pltpu.VMEM((size,) + gram_part.shape, f32),
-            dma((size,)),
-            dma((size,)),
-            dma((deep + 1,)),
-            dma,
+            pltpu.VMEM((4,) + gram_part.shape, f32),
+            pltpu.VMEM((deep,) + gram_part.shape, f32),
+            pltpu.VMEM(gram_part.shape, f32),
+            dma((4,)),
+            dma((4,)),
             dma((deep,)),
             dma((deep,)),
-            dma((2 * deep,)),
-            dma((deep,)),
-            dma((2 * deep,)),
+            dma,
+            dma((2, deep, 2)),
+            dma((2, deep, 2)),
+            dma((deep, 2)),
+            dma((deep, 2)),
+            dma((2, deep, 2)),
+            dma((2, deep, 2)),
         ],
         compiler_params=pltpu.CompilerParams(
             collective_id=0, has_side_effects=True, vmem_limit_bytes=16 * MIB
@@ -212,27 +281,35 @@
     )(x_bf, gram_part)
 
 
-def sum_kernel(size, part_ref, out_ref, buf, send, recv):
+def sum_kernel(size, part_ref, out_ref, plane_buf, line_buf, half_sum, p_send, p_recv, l_send, l_recv):
     me = lax.axis_index("rows")
-    peer_barrier(me, size)
-    copies = []
-    for k in range(1, size):
-        copy = remote(part_ref, buf.at[k], send.at[k], recv.at[k], lax.rem(me + k, size))
-        copy.start()
-        copies.append(copy)
-    for copy in copies:
+    planes, lines = plane_peers(me), line_peers(me, size)
+    peer_barrier(planes + lines)
+    for copy in send_parts(part_ref, plane_buf, p_send, p_recv, planes):
         copy.wait()
-    out_ref[...] = ordered_sum(me, size, part_ref, buf)
+    half_sum[...] = ordered_sum(lax.rem(me, 4), 4, part_ref, plane_buf)
+    for copy in send_parts(half_sum, line_buf, l_send, l_recv, lines):
+        copy.wait()
+    out_ref[...] = ordered_sum(me // 4, size // 4, half_sum, line_buf)
 
 
 def sum_rows(part, size):
     dma = pltpu.SemaphoreType.DMA
+    deep = size // 4
     return pl.pallas_call(
         functools.partial(sum_kernel, size),
         in_specs=[pl.BlockSpec(memory_space=pltpu.VMEM)],
         out_specs=pl.BlockSpec(memory_space=pltpu.VMEM),
         out_shape=jax.ShapeDtypeStruct(part.shape, f32),
-        scratch_shapes=[pltpu.VMEM((size,) + part.shape, f32), dma((size,)), dma((size,))],
+        scratch_shapes=[
+            pltpu.VMEM((4,) + part.shape, f32),
+            pltpu.VMEM((deep,) + part.shape, f32),
+            pltpu.VMEM(part.shape, f32),
+            dma((4,)),
+            dma((4,)),
+            dma((deep,)),
+            dma((deep,)),
+        ],
         compiler_params=pltpu.CompilerParams(
             collective_id=1, has_side_effects=True, vmem_limit_bytes=16 * MIB
         ),
@@ -277,7 +354,11 @@
         for t in range(count):
             slot = step * count + t
             at = pl.ds(pl.multiple_of(src_ref[slot] * edge, edge), edge)
-            products.append(dot(with_ones(xg_ref[slot // slots, :, at]), tiles_ref[t]))
+            if dot is dot_nt:
+                tile = tiles_ref[t]
+            else:
+                tile = tiles_ref[t // slots, (t % slots) * edge : (t % slots + 1) * edge]
+            products.append(dot(with_ones(xg_ref[slot // slots, :, at]), tile))
         for t in range(count):
             far[dst_ref[step * count + t]] += products[t]
 
@@ -308,7 +389,7 @@
     in_specs = [
         pl.BlockSpec((chunk, nodes), lambda i, *_: (i, 0)),
         tile_spec,
-        tile_spec,
+        pl.BlockSpec((count // slots,) + in_tiles.shape[1:], lambda i, *_: (i, 0, 0)),
         whole(xg.shape),
         whole(x.shape),
     ]
@@ -437,18 +518,25 @@
     slots = remote_tiles.shape[1]
     node_total = nodes * size
     live = jnp.arange(slots)[None, :] < remote_count[:, None]
-    packed = remote_row + blocks * jnp.where(live, remote_col, blocks)
-    far_packed = lax.all_to_all(packed, "rows", split_axis=0, concat_axis=0, tiled=True).reshape(-1)
-    in_tiles = lax.all_to_all(remote_tiles, "rows", split_axis=0, concat_axis=0, tiled=True)
-    in_tiles = in_tiles.reshape(-1, edge, edge)
+    numbers = jnp.concatenate([remote_row, jnp.where(live, remote_col, blocks)], axis=1).astype(bf16)
+    numbers = jnp.pad(numbers[:, None, :], ((0, 0), (0, 15), (0, edge - 2 * slots)))
+    slab = jnp.concatenate([remote_tiles.reshape(size, slots * edge, edge), numbers], axis=1)
+    in_tiles = lax.all_to_all(slab, "rows", split_axis=0, concat_axis=0, tiled=True)
+    far = in_tiles[:, slots * edge, : 2 * slots].astype(jnp.int32)
     own_tiles = remote_tiles.reshape(-1, edge, edge)
     own_dst = jnp.where(live, remote_row, blocks).reshape(-1)
-    index = (remote_col.reshape(-1), own_dst, far_packed % blocks, far_packed // blocks)
+    index = (
+        remote_col.reshape(-1),
+        own_dst,
+        far[:, :slots].reshape(-1),
+        far[:, slots:].reshape(-1),
+    )
     dense = dense_local(local_count, local_row, local_col, local_tiles, nodes)
     basis = start_basis
     direction = start_dir
     degree = None
     basis_bf, gram_part = start(basis)
+    dense, basis_bf = lax.optimization_barrier((dense, basis_bf))
     passes = coeffs.shape[0]
     for iteration in range(passes + 1):
         xg, inv = gather_basis(basis_bf, gram_part, size, node_total)

time: 301 us -> 218 us (0.72)
  Pallas kernels: 270 us -> 195 us
  blocking collectives: 13.6 us -> 0 us
  starting transfers between devices: 4.45 us -> 7.53 us
    pallas_call x3, Pallas kernels: 172 us -> 112 us  [gather_basis(): pl.pallas_call(functools.partial(gather_kernel, size, float(node_total)),...]
    pallas_call x3, Pallas kernels: 40.7 us -> 25.5 us  [sum_rows(): pl.pallas_call(functools.partial(sum_kernel, size), in_specs=[pl.BlockSpe...]
    all_to_all x1 -> x0, blocking collectives: 13.6 us -> none  [shards(): lax.all_to_all(packed, 'rows', split_axis=0, concat_axis=0, tiled=True)]
    concatenate x0 -> x3, other arithmetic: none -> 3.83 us  [the longest x1 3.06 us: shards(): jnp.concatenate([remote_tiles.reshape(size, slots * edge, edge), numbers]...]
    all_to_all x1, starting transfers between devices: 4.45 us -> 7.53 us  [shards(): lax.all_to_all(slab, 'rows', split_axis=0, concat_axis=0, tiled=True)]
    unnamed x21 -> x23, local copies, waits for them, and re-layouts: 7.49 us -> 9.12 us
  transfers between devices with their start and end apart: 1 -> 1, of which waited for: 0 -> 0; matrix products, arithmetic and copies ran while one was open for 1% -> 0% of each run, Pallas kernels for 33% -> 32%
where the time goes in v2:
time: 218 us; the launch traced here: 217 us
  Pallas kernels  195 us (89%)
  local copies, waits for them, and re-layouts  9.9 us (5%)
  starting transfers between devices  7.53 us (3%)
  other arithmetic  3.84 us (2%)
    pallas_call x3, Pallas kernels, gather_basis(): pl.pallas_call(functools.partial(gather_kernel, size, float(node_total)),...  112 us
    pallas_call x3, Pallas kernels, apply_operator(): pl.pallas_call(functools.partial(apply_kernel, first, slots), grid_spec=p...  33 us
    pallas_call x3, Pallas kernels, sum_rows(): pl.pallas_call(functools.partial(sum_kernel, size), in_specs=[pl.BlockSpe...  25.5 us
    pallas_call x1, Pallas kernels, dense_local(): pl.pallas_call(functools.partial(dense_kernel, per_step), grid_spec=pltpu...  14.1 us
    pallas_call x3, Pallas kernels, update(): pl.pallas_call(functools.partial(update_kernel, last, float(node_total)),...  9.7 us
    unnamed x23, local copies, waits for them, and re-layouts  9.12 us
    all_to_all x1, starting transfers between devices, shards(): lax.all_to_all(slab, 'rows', split_axis=0, concat_axis=0, tiled=True)  7.53 us
  transfers between devices with their start and end apart: 1, of which 0 were waited for; matrix products, arithmetic and copies ran while one was open for 0% of the time, Pallas kernels for 32%

profile of v2, /device:TPU:0, one launch (start us, length us, event | category | flops | bytes accessed | tf_op | source)
XLA Modules:
  0.0 217.3 jit_solution(16373331786674849109)
XLA Ops:
  0.6 0.8 convert_bitcast_fusion
  1.4 0.1 copy.36
  1.5 3.1 %fusion.1 = bf16[16,528,128]{2,1,0:T(8,128)(2,1)} fusion(bf16[16,1,8]{2,1,0:T(2,128)(2,1)S(1)} %copy.36, bf16[16,512,128]{2,1,0:T(8,128)(2,1)} %bitcast.11), kind=kLoop, calls=%fused_computation.2 | loop fusion | flops 6488064 | bytes 4260096 | tf_op jit(solution)/shard_map/concatenate | solution.py:523
  4.6 7.5 %all-to-all-start = ((bf16[16,528,128]{2,1,0:T(8,128)(2,1)}), bf16[16,528,128]{2,1,0:T(8,128)(2,1)S(1)}, u32[]{:S(2)}, u32[]{:S(2)}) async-start(bf16[16,528,128]{2,1,0:T(8,128)(2,1)} %fusion.1), calls=%async_computation | async-start | bytes 4325376 | tf_op jit(solution)/shard_map/all_to_all | solution.py:524
  12.1 0.1 copy.34
  12.9 0.1 copy.35
  12.9 0.1 reshape.59.own_dst
  13.0 0.1 reshape.58.own_src
  13.1 0.6 start.1
  13.8 0.0 copy-done.8
  13.8 14.1 %dense_local.1.refs_0_ = bf16[2048,2048]{1,0:T(8,128)(2,1)S(1)} custom-call(s32[1]{0:T(128)S(6)} %copy.40.count_ref, s32[256]{0:T(256)S(1)} %copy-done.7, s32[256]{0:T(256)S(1)} %copy-done.8, bf16[256,128,128]{2,1,0:T(8,128)(2,1)} %tiles_ref.1), custom_call_target="tpu_custom_call" | custom-call | flops 1000000000 | bytes 41943040 | tf_op jit(solution)/shard_map/dense_local/pallas_call | solution.py:104
  27.9 3.2 %copy-done = bf16[2048,2048]{1,0:T(8,128)(2,1)} copy-done((bf16[2048,2048]{1,0:T(8,128)(2,1)}, bf16[2048,2048]{1,0:T(8,128)(2,1)S(1)}, u32[]{:S(2)}) %copy-start) | copy-done | bytes 8388632
  31.1 55.0 %gather_basis.3 = (bf16[16,64,2048]{2,1,0:T(8,128)(2,1)S(1)}, f32[64,64]{1,0:T(8,128)S(1)}) custom-call(bf16[64,2048]{1,0:T(8,128)(2,1)S(1)} %get-tuple-element.28.x_ref, f32[32,128]{1,0:T(8,128)S(1)} %get-tuple-element.29.gram_ref), custom_call_target="tpu_custom_call" | custom-call | tf_op jit(solution)/shard_map/gather_basis/pallas_call | solution.py:253
  86.1 2.0 copy-done.4
  88.1 0.1 copy.37
  88.2 0.1 copy.39
  88.3 0.1 reshape.62.in_dst
  88.4 0.1 copy.38
  88.5 0.1 reshape.61.in_src
  88.6 1.6 copy-done.1
  90.2 2.2 %copy-done.5 = bf16[16,64,2048]{2,1,0:T(8,128)(2,1)S(1)} copy-done((bf16[16,64,2048]{2,1,0:T(8,128)(2,1)S(1)}, bf16[16,64,2048]{2,1,0:T(8,128)(2,1)}, u32[]{:S(2)}) %copy-start.5) | copy-done | bytes 4194328
  92.4 11.2 %apply_operator.3 = (f32[64,2048]{1,0:T(8,128)S(1)}, f32[32,128]{1,0:T(8,128)S(1)}, f32[8,2048]{1,0:T(8,128)S(1)}) custom-call(s32[64]{0:T(128)S(1)} %reshape.58.own_src, s32[64]{0:T(128)S(1)} %reshape.59.own_dst, s32[64]{0:T(128)S(1)} %reshape.61.in_src, s32[64]{0:T(128)S(1)} %reshape.62.in_dst, bf16[2048,2048]{1,0:T(8,128)(2,1)} %copy-done, ...), custom_call_target="tpu_custom_call" | custom-call | tf_op jit(solution)/shard_map/apply_operator/pallas_call | solution.py:408
  103.5 8.2 %sum_rows.3.cross_ref = f32[32,128]{1,0:T(8,128)S(1)} custom-call(f32[32,128]{1,0:T(8,128)S(1)} %get-tuple-element.33.part_ref), custom_call_target="tpu_custom_call" | custom-call | tf_op jit(solution)/shard_map/sum_rows/pallas_call | solution.py:299
  111.7 3.2 %update.3 = (f32[64,2048]{1,0:T(8,128)S(1)}, bf16[64,2048]{1,0:T(8,128)(2,1)S(1)}, f32[64,2048]{1,0:T(8,128)S(1)}, f32[32,128]{1,0:T(8,128)S(1)}) custom-call(f32[64,64]{1,0:T(8,128)S(1)} %get-tuple-element.30.inv_ref, f32[32,128]{1,0:T(8,128)S(1)} %sum_rows.3.cross_ref, f32[64,2048]{1,0:T(8,128)S(1)} %get-tuple-element.34.image_ref, ...), custom_call_target="tpu_custom_call" | custom-call | tf_op jit(solution)/shard_map/update/pallas_call | solution.py:469
  115.0 28.6 %gather_basis.4 = (bf16[16,64,2048]{2,1,0:T(8,128)(2,1)S(1)}, f32[64,64]{1,0:T(8,128)S(1)}) custom-call(bf16[64,2048]{1,0:T(8,128)(2,1)S(1)} %get-tuple-element.36.x_ref, f32[32,128]{1,0:T(8,128)S(1)} %get-tuple-element.37.gram_ref), custom_call_target="tpu_custom_call" | custom-call | tf_op jit(solution)/shard_map/gather_basis/pallas_call | solution.py:253
  143.6 11.0 %apply_operator.4 = (f32[64,2048]{1,0:T(8,128)S(1)}, f32[32,128]{1,0:T(8,128)S(1)}) custom-call(s32[64]{0:T(128)S(1)} %reshape.58.own_src, s32[64]{0:T(128)S(1)} %reshape.59.own_dst, s32[64]{0:T(128)S(1)} %reshape.61.in_src, s32[64]{0:T(128)S(1)} %reshape.62.in_dst, bf16[2048,2048]{1,0:T(8,128)(2,1)} %copy-done, bf16[64,128,128]{2,1,0:T(8,128)(2,1)S(1)} %bitcast.13, ...), custom_call_target="tpu_custom_call" | custom-call | tf_op jit(solution)/shard_map/apply_operator/pallas_call | solution.py:408
  154.6 8.5 %sum_rows.4.cross_ref = f32[32,128]{1,0:T(8,128)S(1)} custom-call(f32[32,128]{1,0:T(8,128)S(1)} %get-tuple-element.41.part_ref), custom_call_target="tpu_custom_call" | custom-call | tf_op jit(solution)/shard_map/sum_rows/pallas_call | solution.py:299
  163.1 3.8 %update.4 = (f32[64,2048]{1,0:T(8,128)S(1)}, bf16[64,2048]{1,0:T(8,128)(2,1)S(1)}, f32[64,2048]{1,0:T(8,128)}, f32[32,128]{1,0:T(8,128)S(1)}) custom-call(f32[64,64]{1,0:T(8,128)S(1)} %get-tuple-element.38.inv_ref, f32[32,128]{1,0:T(8,128)S(1)} %sum_rows.4.cross_ref, f32[64,2048]{1,0:T(8,128)S(1)} %get-tuple-element.42.image_ref, ...), custom_call_target="tpu_custom_call" | custom-call | tf_op jit(solution)/shard_map/update/pallas_call | solution.py:469
  166.9 28.1 %gather_basis.5 = (bf16[16,64,2048]{2,1,0:T(8,128)(2,1)S(1)}, f32[64,64]{1,0:T(8,128)S(1)}) custom-call(bf16[64,2048]{1,0:T(8,128)(2,1)S(1)} %get-tuple-element.44.x_ref, f32[32,128]{1,0:T(8,128)S(1)} %get-tuple-element.45.gram_ref), custom_call_target="tpu_custom_call" | custom-call | tf_op jit(solution)/shard_map/gather_basis/pallas_call | solution.py:253
  195.0 10.8 %apply_operator.5 = (f32[64,2048]{1,0:T(8,128)S(1)}, f32[32,128]{1,0:T(8,128)S(1)}) custom-call(s32[64]{0:T(128)S(1)} %reshape.58.own_src, s32[64]{0:T(128)S(1)} %reshape.59.own_dst, s32[64]{0:T(128)S(1)} %reshape.61.in_src, s32[64]{0:T(128)S(1)} %reshape.62.in_dst, bf16[2048,2048]{1,0:T(8,128)(2,1)} %copy-done, bf16[64,128,128]{2,1,0:T(8,128)(2,1)S(1)} %bitcast.14, ...), custom_call_target="tpu_custom_call" | custom-call | tf_op jit(solution)/shard_map/apply_operator/pallas_call | solution.py:408
  205.8 8.9 %sum_rows.5.cross_ref = f32[32,128]{1,0:T(8,128)S(1)} custom-call(f32[32,128]{1,0:T(8,128)S(1)} %get-tuple-element.49.part_ref), custom_call_target="tpu_custom_call" | custom-call | tf_op jit(solution)/shard_map/sum_rows/pallas_call | solution.py:299
  214.7 2.6 %update.5 = (f32[64,2048]{1,0:T(8,128)}, f32[64,2048]{1,0:T(8,128)}, f32[64,64]{1,0:T(8,128)}) custom-call(f32[64,64]{1,0:T(8,128)S(1)} %get-tuple-element.46.inv_ref, f32[32,128]{1,0:T(8,128)S(1)} %sum_rows.5.cross_ref, f32[64,2048]{1,0:T(8,128)S(1)} %get-tuple-element.50.image_ref, f32[64,2048]{1,0:T(8,128)S(1)} %get-tuple-element.48.refs_4_.x_ref, ...), custom_call_target="tpu_custom_call" | custom-call | tf_op jit(solution)/shard_map/update/pallas_call | solution.py:469
  (22 shorter events, 0.1 us)
Async XLA Ops:
  4.6 7.5 %copy-start.10 = (s32[16,4]{0,1:T(4,128)S(1)}, s32[16,4]{0,1:T(4,128)}, u32[]{:S(2)}) copy-start(s32[16,4]{0,1:T(4,128)} %param.17) | copy-start | bytes 772
  4.6 8.6 %copy-start.3 = (f32[64,2048]{1,0:T(8,128)S(1)}, f32[64,2048]{1,0:T(8,128)}, u32[]{:S(2)}) copy-start(f32[64,2048]{1,0:T(8,128)} %x_ref.3) | copy-start | bytes 1572868
  4.6 9.2 %copy-start.7 = (s32[256]{0:T(256)S(1)}, s32[256]{0:T(256)}, u32[]{:S(2)}) copy-start(s32[256]{0:T(256)} %row_ref.1) | copy-start | bytes 3076
  4.6 9.2 %copy-start.8 = (s32[256]{0:T(256)S(1)}, s32[256]{0:T(256)}, u32[]{:S(2)}) copy-start(s32[256]{0:T(256)} %col_ref.1) | copy-start | bytes 3076
  4.6 83.5 %all-to-all-start = ((bf16[16,528,128]{2,1,0:T(8,128)(2,1)}), bf16[16,528,128]{2,1,0:T(8,128)(2,1)S(1)}, u32[]{:S(2)}, u32[]{:S(2)}) async-start(bf16[16,528,128]{2,1,0:T(8,128)(2,1)} %fusion.1), calls=%async_computation | async-start | bytes 4325376 | tf_op jit(solution)/shard_map/all_to_all | solution.py:524
  13.8 74.3 %copy-start.9 = (f32[2,64,192]{2,1,0:T(8,128)S(1)}, f32[2,64,192]{2,1,0:T(8,128)}, u32[]{:S(2)}) copy-start(f32[2,64,192]{2,1,0:T(8,128)} %param.21) | copy-start | bytes 294916
  27.9 3.2 %copy-start = (bf16[2048,2048]{1,0:T(8,128)(2,1)}, bf16[2048,2048]{1,0:T(8,128)(2,1)S(1)}, u32[]{:S(2)}) copy-start(bf16[2048,2048]{1,0:T(8,128)(2,1)S(1)} %dense_local.1.refs_0_) | copy-start | bytes 25165828
  86.1 2.0 copy-start.4
  88.6 1.6 copy-start.1
  90.2 2.2 %copy-start.5 = (bf16[16,64,2048]{2,1,0:T(8,128)(2,1)S(1)}, bf16[16,64,2048]{2,1,0:T(8,128)(2,1)}, u32[]{:S(2)}) copy-start(bf16[16,64,2048]{2,1,0:T(8,128)(2,1)} %copy-done.4) | copy-start | bytes 12582916
  92.4 19.3 %copy-start.6 = (f32[64,2048]{1,0:T(8,128)S(1)}, f32[64,2048]{1,0:T(8,128)}, u32[]{:S(2)}) copy-start(f32[64,2048]{1,0:T(8,128)} %refs_1_.1) | copy-start | bytes 1572868
  92.4 51.2 %copy-start.2 = (bf16[16,4,128,128]{3,2,1,0:T(8,128)(2,1)S(1)}, bf16[16,4,128,128]{3,2,1,0:T(8,128)(2,1)}, u32[]{:S(2)}) copy-start(bf16[16,4,128,128]{3,2,1,0:T(8,128)(2,1)} %param.15) | copy-start | bytes 6291460

commit v3 on v2

--- a/solution.py
+++ b/solution.py
@@ -131,7 +131,7 @@
     return lax.fori_loop(first, last, eliminate, both)
 
 
-def gather_kernel(size, node_total, x_ref, gram_ref, xg_ref, inv_ref, plane_buf, line_buf, half_sum, p_send, p_recv,
+def gather_kernel(size, node_total, x_ref, gram_ref, dense_ref, xg_ref, inv_ref, local_ref, plane_buf, line_buf, half_sum, p_send, p_recv,
                   l_send, l_recv, own_sem, z_send, z_recv, y_send, y_recv, s_send, s_recv):
     me = lax.axis_index("rows")
     deep = size // 4
@@ -151,6 +151,22 @@
     def along(base, k):
         return lax.rem(base + 4 * k + size, size)
 
+    columns, nodes = x_ref.shape
+    ones = jnp.ones((local_ref.shape[0] - columns, nodes), bf16)
+    x_all = jnp.concatenate([x_ref[...], ones], axis=0)
+    turns = 2 * deep
+    chunk = nodes // turns
+
+    def local_turns(first, last):
+        def turn(i, nothing):
+            here = pl.ds(pl.multiple_of(i * chunk, chunk), chunk)
+            x_here = jnp.concatenate([x_ref[:, here], ones[:, :chunk]], axis=0)
+            local_ref[...] += dot_nn(x_here, dense_ref[here, :])
+            local_ref[:, here] += dot_nt(x_all, dense_ref[here, :])
+            return nothing
+
+        lax.fori_loop(first, last, turn, 0)
+
     planes, lines = plane_peers(me), line_peers(me, size)
     peer_barrier(planes + lines)
     plane_copies = send_parts(gram_ref, plane_buf, p_send, p_recv, planes)
@@ -175,6 +191,7 @@
         send(None, remote(src, part(me, h), s_send.at[0, z, h], s_recv.at[0, z, h], sib))
     own = pltpu.make_async_copy(x_ref, xg_ref.at[me], own_sem)
     own.start()
+    local_ref[...] = jnp.zeros_like(local_ref)
 
     for copy in plane_copies:
         copy.wait()
@@ -216,6 +233,7 @@
     n = inv_ref.shape[0]
     rows = lax.broadcasted_iota(jnp.int32, (n, 2 * n), 0)
     lanes = lax.broadcasted_iota(jnp.int32, (n, 2 * n), 1)
+    local_turns(0, 2)
     take_along_z(1)
     for copy in line_copies:
         copy.wait()
@@ -226,6 +244,7 @@
     for k in range(1, deep):
         both = back_substitute(n, cut[k - 1], cut[k], both)
         take_along_y(k - 1)
+        local_turns(2 * k, 2 * k + 2)
         if k + 1 < deep:
             take_along_z(k + 1)
     both = back_substitute(n, cut[deep - 1], cut[deep], both)
@@ -246,17 +265,18 @@
     own.wait()
 
 
-def gather_basis(x_bf, gram_part, size, node_total):
+def gather_basis(x_bf, gram_part, dense, size, node_total):
     columns, nodes = x_bf.shape
     deep = size // 4
     dma = pltpu.SemaphoreType.DMA
     return pl.pallas_call(
         functools.partial(gather_kernel, size, float(node_total)),
-        in_specs=[pl.BlockSpec(memory_space=pl.ANY), pl.BlockSpec(memory_space=pltpu.VMEM)],
-        out_specs=[pl.BlockSpec(memory_space=pl.ANY), pl.BlockSpec(memory_space=pltpu.VMEM)],
+        in_specs=[pl.BlockSpec(memory_space=pltpu.VMEM)] * 3,
+        out_specs=[pl.BlockSpec(memory_space=pl.ANY)] + [pl.BlockSpec(memory_space=pltpu.VMEM)] * 2,
         out_shape=[
             jax.ShapeDtypeStruct((size, columns, nodes), bf16),
             jax.ShapeDtypeStruct((columns, columns), f32),
+            jax.ShapeDtypeStruct((columns + 16, nodes), f32),
         ],
         scratch_shapes=[
             pltpu.VMEM((4,) + gram_part.shape, f32),
@@ -275,10 +295,10 @@
             dma((2, deep, 2)),
         ],
         compiler_params=pltpu.CompilerParams(
-            collective_id=0, has_side_effects=True, vmem_limit_bytes=16 * MIB
+            collective_id=0, has_side_effects=True, vmem_limit_bytes=20 * MIB
         ),
         name="gather_basis",
-    )(x_bf, gram_part)
+    )(x_bf, gram_part, dense)
 
 
 def sum_kernel(size, part_ref, out_ref, plane_buf, line_buf, half_sum, p_send, p_recv, l_send, l_recv):
@@ -319,13 +339,13 @@
 
 def apply_kernel(first, slots, own_src, own_dst, in_src, in_dst, *refs):
     if first:
-        dense_ref, own_ref, in_ref, xg_ref, x_ref, image_ref, cross_ref, degree_ref, acc, far = refs
+        local_ref, own_ref, in_ref, xg_ref, x_ref, image_ref, cross_ref, degree_ref, far = refs
     else:
-        dense_ref, own_ref, in_ref, xg_ref, x_ref, degree_ref, image_ref, cross_ref, acc, far = refs
+        local_ref, own_ref, in_ref, xg_ref, x_ref, degree_ref, image_ref, cross_ref, far = refs
     step = pl.program_id(0)
     columns, nodes = x_ref.shape
+    rows = far.shape[1]
     edge = own_ref.shape[1]
-    chunk = dense_ref.shape[0]
 
     def with_ones(x):
         if first:
@@ -334,15 +354,7 @@
 
     @pl.when(step == 0)
     def _():
-        acc[...] = jnp.zeros_like(acc)
         far[...] = jnp.zeros_like(far)
-
-    x_all = with_ones(x_ref[...].astype(bf16))
-    here = pl.ds(pl.multiple_of(step * chunk, chunk), chunk)
-    x_here = with_ones(x_ref[:, here].astype(bf16))
-    dense = dense_ref[...]
-    acc[...] += dot_nn(x_here, dense)
-    acc[:, here] += dot_nt(x_all, dense)
 
     count = own_ref.shape[0]
     blocks = nodes // edge
@@ -366,7 +378,7 @@
     def _():
         for b in range(blocks):
             at = slice(b * edge, (b + 1) * edge)
-            both = acc[:, at] + far[b]
+            both = local_ref[:rows, at] + far[b]
             if first:
                 degree = 0.5 * both[columns : columns + 1]
                 degree_ref[:, at] = jnp.broadcast_to(degree, (8, edge))
@@ -376,18 +388,17 @@
         cross_ref[...] = fold(dot_nt(image_ref[...], x_ref[...], highest))
 
 
-def apply_operator(first, slots, index, dense, own_tiles, in_tiles, xg, x, degree):
+def apply_operator(first, slots, index, local, own_tiles, in_tiles, xg, x, degree):
     columns, nodes = x.shape
     edge = own_tiles.shape[1]
     steps = 8
-    chunk = nodes // steps
     count = own_tiles.shape[0] // steps
     whole = lambda shape: pl.BlockSpec(shape, lambda i, *_: (0,) * len(shape))
     rows = columns + 16 if first else columns
     tile_spec = pl.BlockSpec((count, edge, edge), lambda i, *_: (i, 0, 0))
     degree_shape = (8, nodes)
     in_specs = [
-        pl.BlockSpec((chunk, nodes), lambda i, *_: (i, 0)),
+        whole(local.shape),
         tile_spec,
         pl.BlockSpec((count // slots,) + in_tiles.shape[1:], lambda i, *_: (i, 0, 0)),
         whole(xg.shape),
@@ -398,7 +409,7 @@
         jax.ShapeDtypeStruct(x.shape, f32),
         jax.ShapeDtypeStruct((columns // 2, 2 * columns), f32),
     ]
-    operands = [dense, own_tiles, in_tiles, xg, x]
+    operands = [local, own_tiles, in_tiles, xg, x]
     if first:
         out_specs.append(whole(degree_shape))
         out_shape.append(jax.ShapeDtypeStruct(degree_shape, f32))
@@ -413,12 +424,11 @@
             in_specs=in_specs,
             out_specs=out_specs,
             scratch_shapes=[
-                pltpu.VMEM((rows, nodes), f32),
                 pltpu.VMEM((nodes // edge + 1, rows, edge), f32),
             ],
         ),
         out_shape=out_shape,
-        compiler_params=pltpu.CompilerParams(vmem_limit_bytes=44 * MIB),
+        compiler_params=pltpu.CompilerParams(vmem_limit_bytes=32 * MIB),
         name="apply_operator",
     )(*index, *operands)
 
@@ -539,8 +549,8 @@
     dense, basis_bf = lax.optimization_barrier((dense, basis_bf))
     passes = coeffs.shape[0]
     for iteration in range(passes + 1):
-        xg, inv = gather_basis(basis_bf, gram_part, size, node_total)
-        out = apply_operator(iteration == 0, slots, index, dense, own_tiles, in_tiles, xg, basis, degree)
+        xg, inv, local = gather_basis(basis_bf, gram_part, dense, size, node_total)
+        out = apply_operator(iteration == 0, slots, index, local, own_tiles, in_tiles, xg, basis, degree)
         image, cross_part = out[:2]
         if iteration == 0:
             degree = out[2]

time: 218 us -> 202 us (0.927)
  Pallas kernels: 195 us -> 182 us
  local copies, waits for them, and re-layouts: 9.9 us -> 6.71 us
    pallas_call x3, Pallas kernels: 33 us -> 13.7 us  [apply_operator(): pl.pallas_call(functools.partial(apply_kernel, first, slots), grid_spec=p...]
    pallas_call x3, Pallas kernels: 112 us -> 116 us  [gather_basis(): pl.pallas_call(functools.partial(gather_kernel, size, float(node_total)),...]
    unnamed x23 -> x25, local copies, waits for them, and re-layouts: 9.12 us -> 5.93 us
    pallas_call x3, Pallas kernels: 25.5 us -> 28 us  [sum_rows(): pl.pallas_call(functools.partial(sum_kernel, size), in_specs=[pl.BlockSpe...]
  transfers between devices with their start and end apart: 1 -> 1, of which waited for: 0 -> 0; matrix products, arithmetic and copies ran while one was open for 0% -> 0% of each run, Pallas kernels for 32% -> 37%
where the time goes in v3:
time: 202 us
  Pallas kernels  182 us (90%)
  starting transfers between devices  7.53 us (4%)
  local copies, waits for them, and re-layouts  6.71 us (3%)
  other arithmetic  3.84 us (2%)
    pallas_call x3, Pallas kernels, gather_basis(): pl.pallas_call(functools.partial(gather_kernel, size, float(node_total)),...  116 us
    pallas_call x3, Pallas kernels, sum_rows(): pl.pallas_call(functools.partial(sum_kernel, size), in_specs=[pl.BlockSpe...  28 us
    pallas_call x1, Pallas kernels, dense_local(): pl.pallas_call(functools.partial(dense_kernel, per_step), grid_spec=pltpu...  14 us
    pallas_call x3, Pallas kernels, apply_operator(): pl.pallas_call(functools.partial(apply_kernel, first, slots), grid_spec=p...  13.7 us
    pallas_call x3, Pallas kernels, update(): pl.pallas_call(functools.partial(update_kernel, last, float(node_total)),...  9.7 us
    all_to_all x1, starting transfers between devices, shards(): lax.all_to_all(slab, 'rows', split_axis=0, concat_axis=0, tiled=True)  7.53 us
    unnamed x25, local copies, waits for them, and re-layouts  5.93 us
  transfers between devices with their start and end apart: 1, of which 0 were waited for; matrix products, arithmetic and copies ran while one was open for 0% of the time, Pallas kernels for 37%

profile of v3, /device:TPU:0, one launch (start us, length us, event | category | flops | bytes accessed | tf_op | source)
XLA Modules:
  0.0 201.8 jit_solution(3235436135722703813)
XLA Ops:
  0.6 0.8 convert_bitcast_fusion
  1.4 0.1 copy.36
  1.5 3.1 %fusion.1 = bf16[16,528,128]{2,1,0:T(8,128)(2,1)} fusion(bf16[16,1,8]{2,1,0:T(2,128)(2,1)S(1)} %copy.36, bf16[16,512,128]{2,1,0:T(8,128)(2,1)} %bitcast.11), kind=kLoop, calls=%fused_computation.2 | loop fusion | flops 6488064 | bytes 4260096 | tf_op jit(solution)/shard_map/concatenate | solution.py:533
  4.6 7.5 %all-to-all-start = ((bf16[16,528,128]{2,1,0:T(8,128)(2,1)}), bf16[16,528,128]{2,1,0:T(8,128)(2,1)S(1)}, u32[]{:S(2)}, u32[]{:S(2)}) async-start(bf16[16,528,128]{2,1,0:T(8,128)(2,1)} %fusion.1), calls=%async_computation | async-start | bytes 4325376 | tf_op jit(solution)/shard_map/all_to_all | solution.py:534
  12.1 0.1 copy.34
  12.9 0.1 copy.35
  12.9 0.1 reshape.59.own_dst
  13.0 0.1 reshape.58.own_src
  13.1 0.6 start.1
  13.8 0.0 copy-done.9
  13.8 14.0 %dense_local.1.dense_ref = bf16[2048,2048]{1,0:T(8,128)(2,1)S(1)} custom-call(s32[1]{0:T(128)S(6)} %copy.40.count_ref, s32[256]{0:T(256)S(1)} %copy-done.8, s32[256]{0:T(256)S(1)} %copy-done.9, bf16[256,128,128]{2,1,0:T(8,128)(2,1)} %tiles_ref.1), custom_call_target="tpu_custom_call" | custom-call | flops 1000000000 | bytes 41943040 | tf_op jit(solution)/shard_map/dense_local/pallas_call | solution.py:104
  27.8 59.5 %gather_basis.3 = (bf16[16,64,2048]{2,1,0:T(8,128)(2,1)S(1)}, f32[64,64]{1,0:T(8,128)S(1)}, f32[80,2048]{1,0:T(8,128)S(1)}) custom-call(bf16[64,2048]{1,0:T(8,128)(2,1)S(1)} %get-tuple-element.31.x_ref, f32[32,128]{1,0:T(8,128)S(1)} %get-tuple-element.32.gram_ref, bf16[2048,2048]{1,0:T(8,128)(2,1)S(1)} %dense_local.1.dense_ref), custom_call_target="tpu_custom_call" | custom-call | tf_op jit(solution)/shard_map/gather_basis/pallas_call | solution.py:272
  87.3 2.0 copy-done.5
  89.3 0.1 copy.37
  89.4 0.1 copy.39
  89.4 0.1 reshape.62.in_dst
  89.5 0.1 copy.38
  89.6 0.1 reshape.61.in_src
  89.7 1.6 copy-done.2
  91.3 2.2 %copy-done.6 = bf16[16,64,2048]{2,1,0:T(8,128)(2,1)S(1)} copy-done((bf16[16,64,2048]{2,1,0:T(8,128)(2,1)S(1)}, bf16[16,64,2048]{2,1,0:T(8,128)(2,1)}, u32[]{:S(2)}) %copy-start.6) | copy-done | bytes 4194328
  93.5 4.7 %apply_operator.3 = (f32[64,2048]{1,0:T(8,128)S(1)}, f32[32,128]{1,0:T(8,128)S(1)}, f32[8,2048]{1,0:T(8,128)S(1)}) custom-call(s32[64]{0:T(128)S(1)} %reshape.58.own_src, s32[64]{0:T(128)S(1)} %reshape.59.own_dst, s32[64]{0:T(128)S(1)} %reshape.61.in_src, s32[64]{0:T(128)S(1)} %reshape.62.in_dst, f32[80,2048]{1,0:T(8,128)S(1)} %get-tuple-element.35.refs_0_, ...), custom_call_target="tpu_custom_call" | custom-call | tf_op jit(solution)/shard_map/apply_operator/pallas_call | solution.py:419
  98.2 8.3 %sum_rows.3.cross_ref = f32[32,128]{1,0:T(8,128)S(1)} custom-call(f32[32,128]{1,0:T(8,128)S(1)} %get-tuple-element.37.part_ref), custom_call_target="tpu_custom_call" | custom-call | tf_op jit(solution)/shard_map/sum_rows/pallas_call | solution.py:319
  106.6 3.2 %update.3 = (f32[64,2048]{1,0:T(8,128)S(1)}, bf16[64,2048]{1,0:T(8,128)(2,1)S(1)}, f32[64,2048]{1,0:T(8,128)S(1)}, f32[32,128]{1,0:T(8,128)S(1)}) custom-call(f32[64,64]{1,0:T(8,128)S(1)} %get-tuple-element.34.inv_ref, f32[32,128]{1,0:T(8,128)S(1)} %sum_rows.3.cross_ref, f32[64,2048]{1,0:T(8,128)S(1)} %get-tuple-element.38.image_ref, ...), custom_call_target="tpu_custom_call" | custom-call | tf_op jit(solution)/shard_map/update/pallas_call | solution.py:479
  109.8 0.1 copy-start.3
  109.9 28.6 %gather_basis.4 = (bf16[16,64,2048]{2,1,0:T(8,128)(2,1)S(1)}, f32[64,64]{1,0:T(8,128)S(1)}, f32[80,2048]{1,0:T(8,128)S(1)}) custom-call(bf16[64,2048]{1,0:T(8,128)(2,1)S(1)} %get-tuple-element.40.x_ref, f32[32,128]{1,0:T(8,128)S(1)} %get-tuple-element.41.gram_ref, bf16[2048,2048]{1,0:T(8,128)(2,1)S(1)} %copy-done.1), custom_call_target="tpu_custom_call" | custom-call | tf_op jit(solution)/shard_map/gather_basis/pallas_call | solution.py:272
  138.5 4.6 %apply_operator.4 = (f32[64,2048]{1,0:T(8,128)S(1)}, f32[32,128]{1,0:T(8,128)S(1)}) custom-call(s32[64]{0:T(128)S(1)} %reshape.58.own_src, s32[64]{0:T(128)S(1)} %reshape.59.own_dst, s32[64]{0:T(128)S(1)} %reshape.61.in_src, s32[64]{0:T(128)S(1)} %reshape.62.in_dst, f32[80,2048]{1,0:T(8,128)S(1)} %get-tuple-element.43.refs_0_, ...), custom_call_target="tpu_custom_call" | custom-call | tf_op jit(solution)/shard_map/apply_operator/pallas_call | solution.py:419
  143.1 9.5 %sum_rows.4.cross_ref = f32[32,128]{1,0:T(8,128)S(1)} custom-call(f32[32,128]{1,0:T(8,128)S(1)} %get-tuple-element.46.part_ref), custom_call_target="tpu_custom_call" | custom-call | tf_op jit(solution)/shard_map/sum_rows/pallas_call | solution.py:319
  152.7 3.8 %update.4 = (f32[64,2048]{1,0:T(8,128)S(1)}, bf16[64,2048]{1,0:T(8,128)(2,1)S(1)}, f32[64,2048]{1,0:T(8,128)}, f32[32,128]{1,0:T(8,128)S(1)}) custom-call(f32[64,64]{1,0:T(8,128)S(1)} %get-tuple-element.42.inv_ref, f32[32,128]{1,0:T(8,128)S(1)} %sum_rows.4.cross_ref, f32[64,2048]{1,0:T(8,128)S(1)} %get-tuple-element.47.image_ref, ...), custom_call_target="tpu_custom_call" | custom-call | tf_op jit(solution)/shard_map/update/pallas_call | solution.py:479
  156.5 28.1 %gather_basis.5 = (bf16[16,64,2048]{2,1,0:T(8,128)(2,1)S(1)}, f32[64,64]{1,0:T(8,128)S(1)}, f32[80,2048]{1,0:T(8,128)S(1)}) custom-call(bf16[64,2048]{1,0:T(8,128)(2,1)S(1)} %get-tuple-element.49.x_ref, f32[32,128]{1,0:T(8,128)S(1)} %get-tuple-element.50.gram_ref, bf16[2048,2048]{1,0:T(8,128)(2,1)S(1)} %copy-done.1), custom_call_target="tpu_custom_call" | custom-call | tf_op jit(solution)/shard_map/gather_basis/pallas_call | solution.py:272
  184.6 4.4 %apply_operator.5 = (f32[64,2048]{1,0:T(8,128)S(1)}, f32[32,128]{1,0:T(8,128)S(1)}) custom-call(s32[64]{0:T(128)S(1)} %reshape.58.own_src, s32[64]{0:T(128)S(1)} %reshape.59.own_dst, s32[64]{0:T(128)S(1)} %reshape.61.in_src, s32[64]{0:T(128)S(1)} %reshape.62.in_dst, f32[80,2048]{1,0:T(8,128)S(1)} %get-tuple-element.52.refs_0_, ...), custom_call_target="tpu_custom_call" | custom-call | tf_op jit(solution)/shard_map/apply_operator/pallas_call | solution.py:419
  189.0 10.1 %sum_rows.5.cross_ref = f32[32,128]{1,0:T(8,128)S(1)} custom-call(f32[32,128]{1,0:T(8,128)S(1)} %get-tuple-element.55.part_ref), custom_call_target="tpu_custom_call" | custom-call | tf_op jit(solution)/shard_map/sum_rows/pallas_call | solution.py:319
  199.1 2.6 %update.5 = (f32[64,2048]{1,0:T(8,128)}, f32[64,2048]{1,0:T(8,128)}, f32[64,64]{1,0:T(8,128)}) custom-call(f32[64,64]{1,0:T(8,128)S(1)} %get-tuple-element.51.inv_ref, f32[32,128]{1,0:T(8,128)S(1)} %sum_rows.5.cross_ref, f32[64,2048]{1,0:T(8,128)S(1)} %get-tuple-element.56.image_ref, f32[64,2048]{1,0:T(8,128)S(1)} %get-tuple-element.54.refs_4_.x_ref, ...), custom_call_target="tpu_custom_call" | custom-call | tf_op jit(solution)/shard_map/update/pallas_call | solution.py:479
  (24 shorter events, 0.1 us)
Async XLA Ops:
  4.6 7.5 %copy-start.11 = (s32[16,4]{0,1:T(4,128)S(1)}, s32[16,4]{0,1:T(4,128)}, u32[]{:S(2)}) copy-start(s32[16,4]{0,1:T(4,128)} %param.17) | copy-start | bytes 772
  4.6 8.6 %copy-start.4 = (f32[64,2048]{1,0:T(8,128)S(1)}, f32[64,2048]{1,0:T(8,128)}, u32[]{:S(2)}) copy-start(f32[64,2048]{1,0:T(8,128)} %x_ref.3) | copy-start | bytes 1572868
  4.6 9.2 %copy-start.8 = (s32[256]{0:T(256)S(1)}, s32[256]{0:T(256)}, u32[]{:S(2)}) copy-start(s32[256]{0:T(256)} %row_ref.1) | copy-start | bytes 3076
  4.6 9.2 %copy-start.9 = (s32[256]{0:T(256)S(1)}, s32[256]{0:T(256)}, u32[]{:S(2)}) copy-start(s32[256]{0:T(256)} %col_ref.1) | copy-start | bytes 3076
  4.6 84.7 %all-to-all-start = ((bf16[16,528,128]{2,1,0:T(8,128)(2,1)}), bf16[16,528,128]{2,1,0:T(8,128)(2,1)S(1)}, u32[]{:S(2)}, u32[]{:S(2)}) async-start(bf16[16,528,128]{2,1,0:T(8,128)(2,1)} %fusion.1), calls=%async_computation | async-start | bytes 4325376 | tf_op jit(solution)/shard_map/all_to_all | solution.py:534
  27.7 59.5 %copy-start = (bf16[2048,2048]{1,0:T(8,128)(2,1)}, bf16[2048,2048]{1,0:T(8,128)(2,1)S(1)}, u32[]{:S(2)}) copy-start(bf16[2048,2048]{1,0:T(8,128)(2,1)S(1)} %dense_local.1.dense_ref) | copy-start | bytes 25165828
  27.8 61.5 %copy-start.10 = (f32[2,64,192]{2,1,0:T(8,128)S(1)}, f32[2,64,192]{2,1,0:T(8,128)}, u32[]{:S(2)}) copy-start(f32[2,64,192]{2,1,0:T(8,128)} %param.21) | copy-start | bytes 294916
  87.2 2.0 copy-start.5
  89.7 1.6 copy-start.2
  91.3 2.2 %copy-start.6 = (bf16[16,64,2048]{2,1,0:T(8,128)(2,1)S(1)}, bf16[16,64,2048]{2,1,0:T(8,128)(2,1)}, u32[]{:S(2)}) copy-start(bf16[16,64,2048]{2,1,0:T(8,128)(2,1)} %copy-done.5) | copy-start | bytes 12582916
  93.5 13.1 %copy-start.7 = (f32[64,2048]{1,0:T(8,128)S(1)}, f32[64,2048]{1,0:T(8,128)}, u32[]{:S(2)}) copy-start(f32[64,2048]{1,0:T(8,128)} %refs_1_.1) | copy-start | bytes 1572868
  93.5 16.3 %copy-start.1 = (bf16[2048,2048]{1,0:T(8,128)(2,1)S(1)}, bf16[2048,2048]{1,0:T(8,128)(2,1)}, u32[]{:S(2)}) copy-start(bf16[2048,2048]{1,0:T(8,128)(2,1)} %copy-done) | copy-start | bytes 25165828
  109.8 28.7 %copy-start.3 = (bf16[16,4,128,128]{3,2,1,0:T(8,128)(2,1)S(1)}, bf16[16,4,128,128]{3,2,1,0:T(8,128)(2,1)}, u32[]{:S(2)}) copy-start(bf16[16,4,128,128]{3,2,1,0:T(8,128)(2,1)} %param.15) | copy-start | bytes 6291460

commit v4 on v3

--- a/solution.py
+++ b/solution.py
@@ -142,7 +142,7 @@
     ynb = me + 2 - 4 * mid
     other = sib + 2 - 4 * mid
     up, down = lax.rem(me + 4, size), lax.rem(me - 4 + size, size)
-    pieces = 2
+    pieces = 4
     piece = x_ref.shape[0] // pieces
 
     def part(block, h):
@@ -287,12 +287,12 @@
             dma((deep,)),
             dma((deep,)),
             dma,
-            dma((2, deep, 2)),
-            dma((2, deep, 2)),
-            dma((deep, 2)),
-            dma((deep, 2)),
-            dma((2, deep, 2)),
-            dma((2, deep, 2)),
+            dma((2, deep, 4)),
+            dma((2, deep, 4)),
+            dma((deep, 4)),
+            dma((deep, 4)),
+            dma((2, deep, 4)),
+            dma((2, deep, 4)),
         ],
         compiler_params=pltpu.CompilerParams(
             collective_id=0, has_side_effects=True, vmem_limit_bytes=20 * MIB

time: 202 us -> 204 us (level)
    pallas_call x3, Pallas kernels: 116 us -> 119 us  [gather_basis(): pl.pallas_call(functools.partial(gather_kernel, size, float(node_total)),...]
where the time goes in v4:
time: 204 us; the launch traced here: 203 us
  Pallas kernels  184 us (90%)
  starting transfers between devices  7.53 us (4%)
  local copies, waits for them, and re-layouts  6.71 us (3%)
  other arithmetic  3.84 us (2%)
    pallas_call x3, Pallas kernels, gather_basis(): pl.pallas_call(functools.partial(gather_kernel, size, float(node_total)),...  119 us
    pallas_call x3, Pallas kernels, sum_rows(): pl.pallas_call(functools.partial(sum_kernel, size), in_specs=[pl.BlockSpe...  28.1 us
    pallas_call x3, Pallas kernels, apply_operator(): pl.pallas_call(functools.partial(apply_kernel, first, slots), grid_spec=p...  13.5 us
    pallas_call x1, Pallas kernels, dense_local(): pl.pallas_call(functools.partial(dense_kernel, per_step), grid_spec=pltpu...  12.8 us
    pallas_call x3, Pallas kernels, update(): pl.pallas_call(functools.partial(update_kernel, last, float(node_total)),...  9.7 us
    all_to_all x1, starting transfers between devices, shards(): lax.all_to_all(slab, 'rows', split_axis=0, concat_axis=0, tiled=True)  7.53 us
    unnamed x25, local copies, waits for them, and re-layouts  5.93 us
  transfers between devices with their start and end apart: 1, of which 0 were waited for; matrix products, arithmetic and copies ran while one was open for 0% of the time, Pallas kernels for 37%

profile of v4, /device:TPU:0, one launch (start us, length us, event | category | flops | bytes accessed | tf_op | source)
XLA Modules:
  0.0 203.3 jit_solution(3503730562186777657)
XLA Ops:
  0.6 0.8 convert_bitcast_fusion
  1.4 0.1 copy.36
  1.5 3.1 %fusion.1 = bf16[16,528,128]{2,1,0:T(8,128)(2,1)} fusion(bf16[16,1,8]{2,1,0:T(2,128)(2,1)S(1)} %copy.36, bf16[16,512,128]{2,1,0:T(8,128)(2,1)} %bitcast.11), kind=kLoop, calls=%fused_computation.2 | loop fusion | flops 6488064 | bytes 4260096 | tf_op jit(solution)/shard_map/concatenate | solution.py:533
  4.6 7.5 %all-to-all-start = ((bf16[16,528,128]{2,1,0:T(8,128)(2,1)}), bf16[16,528,128]{2,1,0:T(8,128)(2,1)S(1)}, u32[]{:S(2)}, u32[]{:S(2)}) async-start(bf16[16,528,128]{2,1,0:T(8,128)(2,1)} %fusion.1), calls=%async_computation | async-start | bytes 4325376 | tf_op jit(solution)/shard_map/all_to_all | solution.py:534
  12.1 0.1 copy.34
  12.9 0.1 copy.35
  12.9 0.1 reshape.59.own_dst
  13.0 0.1 reshape.58.own_src
  13.1 0.6 start.1
  13.8 0.0 copy-done.9
  13.8 12.8 %dense_local.1.dense_ref = bf16[2048,2048]{1,0:T(8,128)(2,1)S(1)} custom-call(s32[1]{0:T(128)S(6)} %copy.40.count_ref, s32[256]{0:T(256)S(1)} %copy-done.8, s32[256]{0:T(256)S(1)} %copy-done.9, bf16[256,128,128]{2,1,0:T(8,128)(2,1)} %tiles_ref.1), custom_call_target="tpu_custom_call" | custom-call | flops 1000000000 | bytes 41943040 | tf_op jit(solution)/shard_map/dense_local/pallas_call | solution.py:104
  26.6 61.3 %gather_basis.3 = (bf16[16,64,2048]{2,1,0:T(8,128)(2,1)S(1)}, f32[64,64]{1,0:T(8,128)S(1)}, f32[80,2048]{1,0:T(8,128)S(1)}) custom-call(bf16[64,2048]{1,0:T(8,128)(2,1)S(1)} %get-tuple-element.31.x_ref, f32[32,128]{1,0:T(8,128)S(1)} %get-tuple-element.32.gram_ref, bf16[2048,2048]{1,0:T(8,128)(2,1)S(1)} %dense_local.1.dense_ref), custom_call_target="tpu_custom_call" | custom-call | tf_op jit(solution)/shard_map/gather_basis/pallas_call | solution.py:272
  87.9 2.0 copy-done.5
  89.9 0.1 copy.37
  90.0 0.1 copy.39
  90.1 0.1 reshape.62.in_dst
  90.2 0.1 copy.38
  90.3 0.1 reshape.61.in_src
  90.4 1.6 copy-done.2
  92.0 2.2 %copy-done.6 = bf16[16,64,2048]{2,1,0:T(8,128)(2,1)S(1)} copy-done((bf16[16,64,2048]{2,1,0:T(8,128)(2,1)S(1)}, bf16[16,64,2048]{2,1,0:T(8,128)(2,1)}, u32[]{:S(2)}) %copy-start.6) | copy-done | bytes 4194328
  94.1 4.7 %apply_operator.3 = (f32[64,2048]{1,0:T(8,128)S(1)}, f32[32,128]{1,0:T(8,128)S(1)}, f32[8,2048]{1,0:T(8,128)S(1)}) custom-call(s32[64]{0:T(128)S(1)} %reshape.58.own_src, s32[64]{0:T(128)S(1)} %reshape.59.own_dst, s32[64]{0:T(128)S(1)} %reshape.61.in_src, s32[64]{0:T(128)S(1)} %reshape.62.in_dst, f32[80,2048]{1,0:T(8,128)S(1)} %get-tuple-element.35.refs_0_, ...), custom_call_target="tpu_custom_call" | custom-call | tf_op jit(solution)/shard_map/apply_operator/pallas_call | solution.py:419
  98.9 8.0 %sum_rows.3.cross_ref = f32[32,128]{1,0:T(8,128)S(1)} custom-call(f32[32,128]{1,0:T(8,128)S(1)} %get-tuple-element.37.part_ref), custom_call_target="tpu_custom_call" | custom-call | tf_op jit(solution)/shard_map/sum_rows/pallas_call | solution.py:319
  106.9 3.3 %update.3 = (f32[64,2048]{1,0:T(8,128)S(1)}, bf16[64,2048]{1,0:T(8,128)(2,1)S(1)}, f32[64,2048]{1,0:T(8,128)S(1)}, f32[32,128]{1,0:T(8,128)S(1)}) custom-call(f32[64,64]{1,0:T(8,128)S(1)} %get-tuple-element.34.inv_ref, f32[32,128]{1,0:T(8,128)S(1)} %sum_rows.3.cross_ref, f32[64,2048]{1,0:T(8,128)S(1)} %get-tuple-element.38.image_ref, ...), custom_call_target="tpu_custom_call" | custom-call | tf_op jit(solution)/shard_map/update/pallas_call | solution.py:479
  110.2 0.1 copy-start.3
  110.2 29.0 %gather_basis.4 = (bf16[16,64,2048]{2,1,0:T(8,128)(2,1)S(1)}, f32[64,64]{1,0:T(8,128)S(1)}, f32[80,2048]{1,0:T(8,128)S(1)}) custom-call(bf16[64,2048]{1,0:T(8,128)(2,1)S(1)} %get-tuple-element.40.x_ref, f32[32,128]{1,0:T(8,128)S(1)} %get-tuple-element.41.gram_ref, bf16[2048,2048]{1,0:T(8,128)(2,1)S(1)} %copy-done.1), custom_call_target="tpu_custom_call" | custom-call | tf_op jit(solution)/shard_map/gather_basis/pallas_call | solution.py:272
  139.2 4.4 %apply_operator.4 = (f32[64,2048]{1,0:T(8,128)S(1)}, f32[32,128]{1,0:T(8,128)S(1)}) custom-call(s32[64]{0:T(128)S(1)} %reshape.58.own_src, s32[64]{0:T(128)S(1)} %reshape.59.own_dst, s32[64]{0:T(128)S(1)} %reshape.61.in_src, s32[64]{0:T(128)S(1)} %reshape.62.in_dst, f32[80,2048]{1,0:T(8,128)S(1)} %get-tuple-element.43.refs_0_, ...), custom_call_target="tpu_custom_call" | custom-call | tf_op jit(solution)/shard_map/apply_operator/pallas_call | solution.py:419
  143.6 10.3 %sum_rows.4.cross_ref = f32[32,128]{1,0:T(8,128)S(1)} custom-call(f32[32,128]{1,0:T(8,128)S(1)} %get-tuple-element.46.part_ref), custom_call_target="tpu_custom_call" | custom-call | tf_op jit(solution)/shard_map/sum_rows/pallas_call | solution.py:319
  154.0 3.8 %update.4 = (f32[64,2048]{1,0:T(8,128)S(1)}, bf16[64,2048]{1,0:T(8,128)(2,1)S(1)}, f32[64,2048]{1,0:T(8,128)}, f32[32,128]{1,0:T(8,128)S(1)}) custom-call(f32[64,64]{1,0:T(8,128)S(1)} %get-tuple-element.42.inv_ref, f32[32,128]{1,0:T(8,128)S(1)} %sum_rows.4.cross_ref, f32[64,2048]{1,0:T(8,128)S(1)} %get-tuple-element.47.image_ref, ...), custom_call_target="tpu_custom_call" | custom-call | tf_op jit(solution)/shard_map/update/pallas_call | solution.py:479
  157.8 28.7 %gather_basis.5 = (bf16[16,64,2048]{2,1,0:T(8,128)(2,1)S(1)}, f32[64,64]{1,0:T(8,128)S(1)}, f32[80,2048]{1,0:T(8,128)S(1)}) custom-call(bf16[64,2048]{1,0:T(8,128)(2,1)S(1)} %get-tuple-element.49.x_ref, f32[32,128]{1,0:T(8,128)S(1)} %get-tuple-element.50.gram_ref, bf16[2048,2048]{1,0:T(8,128)(2,1)S(1)} %copy-done.1), custom_call_target="tpu_custom_call" | custom-call | tf_op jit(solution)/shard_map/gather_basis/pallas_call | solution.py:272
  186.6 4.4 %apply_operator.5 = (f32[64,2048]{1,0:T(8,128)S(1)}, f32[32,128]{1,0:T(8,128)S(1)}) custom-call(s32[64]{0:T(128)S(1)} %reshape.58.own_src, s32[64]{0:T(128)S(1)} %reshape.59.own_dst, s32[64]{0:T(128)S(1)} %reshape.61.in_src, s32[64]{0:T(128)S(1)} %reshape.62.in_dst, f32[80,2048]{1,0:T(8,128)S(1)} %get-tuple-element.52.refs_0_, ...), custom_call_target="tpu_custom_call" | custom-call | tf_op jit(solution)/shard_map/apply_operator/pallas_call | solution.py:419
  191.0 9.7 %sum_rows.5.cross_ref = f32[32,128]{1,0:T(8,128)S(1)} custom-call(f32[32,128]{1,0:T(8,128)S(1)} %get-tuple-element.55.part_ref), custom_call_target="tpu_custom_call" | custom-call | tf_op jit(solution)/shard_map/sum_rows/pallas_call | solution.py:319
  200.7 2.6 %update.5 = (f32[64,2048]{1,0:T(8,128)}, f32[64,2048]{1,0:T(8,128)}, f32[64,64]{1,0:T(8,128)}) custom-call(f32[64,64]{1,0:T(8,128)S(1)} %get-tuple-element.51.inv_ref, f32[32,128]{1,0:T(8,128)S(1)} %sum_rows.5.cross_ref, f32[64,2048]{1,0:T(8,128)S(1)} %get-tuple-element.56.image_ref, f32[64,2048]{1,0:T(8,128)S(1)} %get-tuple-element.54.refs_4_.x_ref, ...), custom_call_target="tpu_custom_call" | custom-call | tf_op jit(solution)/shard_map/update/pallas_call | solution.py:479
  (24 shorter events, 0.1 us)
Async XLA Ops:
  4.6 7.5 %copy-start.11 = (s32[16,4]{0,1:T(4,128)S(1)}, s32[16,4]{0,1:T(4,128)}, u32[]{:S(2)}) copy-start(s32[16,4]{0,1:T(4,128)} %param.17) | copy-start | bytes 772
  4.6 8.6 %copy-start.4 = (f32[64,2048]{1,0:T(8,128)S(1)}, f32[64,2048]{1,0:T(8,128)}, u32[]{:S(2)}) copy-start(f32[64,2048]{1,0:T(8,128)} %x_ref.3) | copy-start | bytes 1572868
  4.6 9.2 %copy-start.8 = (s32[256]{0:T(256)S(1)}, s32[256]{0:T(256)}, u32[]{:S(2)}) copy-start(s32[256]{0:T(256)} %row_ref.1) | copy-start | bytes 3076
  4.6 9.2 %copy-start.9 = (s32[256]{0:T(256)S(1)}, s32[256]{0:T(256)}, u32[]{:S(2)}) copy-start(s32[256]{0:T(256)} %col_ref.1) | copy-start | bytes 3076
  4.6 85.3 %all-to-all-start = ((bf16[16,528,128]{2,1,0:T(8,128)(2,1)}), bf16[16,528,128]{2,1,0:T(8,128)(2,1)S(1)}, u32[]{:S(2)}, u32[]{:S(2)}) async-start(bf16[16,528,128]{2,1,0:T(8,128)(2,1)} %fusion.1), calls=%async_computation | async-start | bytes 4325376 | tf_op jit(solution)/shard_map/all_to_all | solution.py:534
  26.6 61.3 %copy-start = (bf16[2048,2048]{1,0:T(8,128)(2,1)}, bf16[2048,2048]{1,0:T(8,128)(2,1)S(1)}, u32[]{:S(2)}) copy-start(bf16[2048,2048]{1,0:T(8,128)(2,1)S(1)} %dense_local.1.dense_ref) | copy-start | bytes 25165828
  26.6 63.3 %copy-start.10 = (f32[2,64,192]{2,1,0:T(8,128)S(1)}, f32[2,64,192]{2,1,0:T(8,128)}, u32[]{:S(2)}) copy-start(f32[2,64,192]{2,1,0:T(8,128)} %param.21) | copy-start | bytes 294916
  87.9 2.0 copy-start.5
  90.4 1.6 copy-start.2
  92.0 2.2 %copy-start.6 = (bf16[16,64,2048]{2,1,0:T(8,128)(2,1)S(1)}, bf16[16,64,2048]{2,1,0:T(8,128)(2,1)}, u32[]{:S(2)}) copy-start(bf16[16,64,2048]{2,1,0:T(8,128)(2,1)} %copy-done.5) | copy-start | bytes 12582916
  94.1 12.7 %copy-start.7 = (f32[64,2048]{1,0:T(8,128)S(1)}, f32[64,2048]{1,0:T(8,128)}, u32[]{:S(2)}) copy-start(f32[64,2048]{1,0:T(8,128)} %refs_1_.1) | copy-start | bytes 1572868
  94.1 16.0 %copy-start.1 = (bf16[2048,2048]{1,0:T(8,128)(2,1)S(1)}, bf16[2048,2048]{1,0:T(8,128)(2,1)}, u32[]{:S(2)}) copy-start(bf16[2048,2048]{1,0:T(8,128)(2,1)} %copy-done) | copy-start | bytes 25165828
  110.2 29.1 %copy-start.3 = (bf16[16,4,128,128]{3,2,1,0:T(8,128)(2,1)S(1)}, bf16[16,4,128,128]{3,2,1,0:T(8,128)(2,1)}, u32[]{:S(2)}) copy-start(bf16[16,4,128,128]{3,2,1,0:T(8,128)(2,1)} %param.15) | copy-start | bytes 6291460
